TPU v7x, 256 devices: a whole 4x4x8 slice. The times are simulated.
256 devices in a mesh: mem: 8 (over y, core), tile: 32 (over z, x).
Axes of the slice: x: 4, y: 4, z: 8, core: 2. Of those that a mesh axis runs over, the one named last changes fastest.
Arguments:
- members: bfloat16 [8, 8, 1024, 2048], P('mem', None, 'tile'), may hold values from -6 to 6
- increment: float32 [8, 1024, 2048], P('mem', 'tile'), may hold values from -6 to 6
- weights: float32 [16], replicated, may hold values from 0.25 to 4
Outputs:
- applied: float32 [8, 1024, 2048], P('mem', 'tile')
All inputs are finite; a program needn't handle non-finite values.
Results may differ from a plain program's by a relative error of at most 0.0017.
Values may be sent and summed in bfloat16 or wider, within the bound.
A program may use at most 64 MiB of HBM per device.

v0:
```python
import jax
import jax.numpy as jnp
from jax import lax
from jax.sharding import PartitionSpec as P

M_DEV = 1
LVLS = 5


lift_first = -1.586134342059924
lift_second = -0.052980118572961
lift_third = 0.882911075530934
lift_fourth = 0.443506852043971
scale_kappa = 1.149604398860241


def passed_along(value, axis, steps):
    count = lax.axis_size(axis)
    pairs = [(source, (source + steps) % count) for source in range(count)]
    return lax.ppermute(value, axis, pairs)


def forward_lift(even_part, odd_part, step_after, step_before):
    odd_part = odd_part + lift_first * (even_part + step_after(even_part))
    even_part = even_part + lift_second * (step_before(odd_part) + odd_part)
    odd_part = odd_part + lift_third * (even_part + step_after(even_part))
    even_part = even_part + lift_fourth * (step_before(odd_part) + odd_part)
    return (even_part * scale_kappa, odd_part / scale_kappa)


def inverse_lift(low_part, high_part, step_after, step_before):
    even_part = low_part / scale_kappa
    odd_part = high_part * scale_kappa
    even_part = even_part - lift_fourth * (step_before(odd_part) + odd_part)
    odd_part = odd_part - lift_third * (even_part + step_after(even_part))
    even_part = even_part - lift_second * (step_before(odd_part) + odd_part)
    odd_part = odd_part - lift_first * (even_part + step_after(even_part))
    return (even_part, odd_part)


def band_next_rows(values):
    incoming = passed_along(values[:, :1], "tile", -1)
    return jnp.concatenate((values[:, 1:], incoming), axis=1)


def band_prior_rows(values):
    incoming = passed_along(values[:, -1:], "tile", 1)
    return jnp.concatenate((incoming, values[:, :-1]), axis=1)


def band_forward(even_part, odd_part):
    return forward_lift(even_part, odd_part, band_next_rows, band_prior_rows)


def band_inverse(low_part, high_part):
    return inverse_lift(low_part, high_part, band_next_rows, band_prior_rows)


def column_next(values):
    return jnp.roll(values, -1, axis=-1)


def column_prior(values):
    return jnp.roll(values, 1, axis=-1)


def split_columns(values):
    return forward_lift(values[..., 0::2], values[..., 1::2], column_next, column_prior)


def join_columns(low_part, high_part):
    even_part, odd_part = inverse_lift(low_part, high_part, column_next, column_prior)
    merged = jnp.stack((even_part, odd_part), axis=-1)
    return merged.reshape(even_part.shape[:-1] + (2 * even_part.shape[-1],))


def analysis_level(approx, row_forward):
    low_rows, high_rows = row_forward(approx[:, 0::2], approx[:, 1::2])
    low_low, low_high = split_columns(low_rows)
    high_low, high_high = split_columns(high_rows)
    return (low_low, jnp.stack((low_high, high_low, high_high), axis=1))


def synthesis_level(approx, detail, row_inverse):
    low_rows = join_columns(approx, detail[:, 0])
    high_rows = join_columns(detail[:, 1], detail[:, 2])
    even_part, odd_part = row_inverse(low_rows, high_rows)
    merged = jnp.stack((even_part, odd_part), axis=2)
    return merged.reshape((merged.shape[0], 2 * merged.shape[1], merged.shape[3]))


def analyze_levels(approx, level_count, row_forward):
    details = []
    for level_index in range(level_count):
        approx, detail = analysis_level(approx, row_forward)
        details.append(detail)
    return (approx, tuple(details))


def synthesize(approx, details, row_inverse):
    for detail in reversed(details):
        approx = synthesis_level(approx, detail, row_inverse)
    return approx


def local(members, increment, weights):
    rows_here = members.shape[2]
    column_count = members.shape[3]
    level_count = members.shape[1]
    stacked = members.reshape((-1, rows_here, column_count)).astype(jnp.float32)
    member_rows = stacked.shape[0]
    stacked_field = jnp.concatenate((stacked, increment), axis=0)
    approx, details = analyze_levels(stacked_field, LVLS, band_forward)

    def fold_members(coefficient):
        member_part = coefficient[:member_rows]
        squared = member_part * member_part
        return jnp.sum(squared.reshape((-1, level_count) + squared.shape[1:]), axis=0)

    energy = (fold_members(approx),) + tuple((fold_members(detail) for detail in details))
    energy = lax.psum_scatter(energy, "mem", scatter_dimension=0, tiled=True)
    scale_members = 1.0 / (M_DEV * lax.axis_size("mem") - 1)
    product_approx = weights[3 * LVLS] * scale_members * energy[0] * approx[member_rows:]
    products = tuple(
        (
            (weights[3 * level_index : 3 * level_index + 3] * scale_members).reshape((1, 3, 1, 1))
            * energy[level_index + 1]
            * details[level_index][member_rows:]
            for level_index in range(LVLS)
        )
    )
    result = synthesize(product_approx, products, band_inverse)
    return result


def solution(mesh):
    return jax.shard_map(
        local,
        mesh=mesh,
        in_specs=(P("mem", None, "tile", None), P("mem", "tile", None), P()),
        out_specs=P("mem", "tile", None),
        check_vma=False,
    )
```

profile of v0, /device:TPU:102, one launch (start us, length us, event | category | flops | bytes accessed | tf_op | source)
XLA Modules:
  0.0 481.7 jit_solution(2739972570210938984)
XLA Ops:
  10.3 3.4 slice.905
  13.9 3.6 collective-permute-done
  18.8 2.1 collective-permute-start.1
  20.9 2.3 collective-permute-done.1
  27.5 4.6 collective-permute-done.2
  32.1 2.3 broadcast_multiply_fusion
  34.3 22.8 %slice.1151 = f32[9,16,1024]{2,1,0:T(8,128)S(1)} slice(f32[9,16,2048]{2,1,0:T(8,128)} %get-tuple-element.67), slice={[0:9:1], [0:16:1], [0:2048:2]} | slice | bytes 1179648 | tf_op jit(solution)/shard_map/slice | solution.py:68
  57.2 22.8 %slice.1152 = f32[9,16,1024]{2,1,0:T(8,128)S(1)} slice(f32[9,16,2048]{2,1,0:T(8,128)} %get-tuple-element.67), slice={[0:9:1], [0:16:1], [1:2048:2]} | slice | bytes 1179648 | tf_op jit(solution)/shard_map/slice | solution.py:68
  81.1 2.3 collective-permute-start.3
  87.1 22.9 %slice.914 = f32[9,16,1024]{2,1,0:T(8,128)S(1)} slice(f32[9,16,2048]{2,1,0:T(8,128)} %fusion.8), slice={[0:9:1], [0:16:1], [0:2048:2]} | slice | bytes 1179648 | tf_op jit(solution)/shard_map/slice | solution.py:68
  110.0 22.0 %slice.915 = f32[9,16,1024]{2,1,0:T(8,128)S(1)} slice(f32[9,16,2048]{2,1,0:T(8,128)S(1)} %copy-done.3), slice={[0:9:1], [0:16:1], [1:2048:2]} | slice | bytes 1179648 | tf_op jit(solution)/shard_map/slice | solution.py:68
  137.6 5.3 %collective-permute-done.4 = f32[9,1,1024]{2,1,0:T(1,128)} collective-permute-done((f32[9,1,1024]{2,1,0:T(1,128)}, f32[9,1,1024]{2,1,0:T(1,128)}, u32[]{:S(2)}, u32[]{:S(2)}) %collective-permute-start.4) | collective-permute-done | bytes 36896 | tf_op jit(solution)/shard_map/ppermute | solution.py:20
  143.8 2.1 collective-permute-start.5
  149.7 5.9 %collective-permute-done.6 = f32[9,1,1024]{2,1,0:T(1,128)S(1)} collective-permute-done((f32[9,1,1024]{2,1,0:T(1,128)S(1)}, f32[9,1,1024]{2,1,0:T(1,128)S(1)}, u32[]{:S(2)}, u32[]{:S(2)}) %collective-permute-start.6) | collective-permute-done | bytes 36896 | tf_op jit(solution)/shard_map/ppermute | solution.py:20
  155.7 5.7 %slice.1111 = f32[9,8,512]{2,1,0:T(8,128)S(1)} slice(f32[9,8,1024]{2,1,0:T(8,128)S(1)} %get-tuple-element.61), slice={[0:9:1], [0:8:1], [0:1024:2]} | slice | bytes 294912 | tf_op jit(solution)/shard_map/slice | solution.py:68
  161.4 5.7 %slice.1112 = f32[9,8,512]{2,1,0:T(8,128)S(1)} slice(f32[9,8,1024]{2,1,0:T(8,128)S(1)} %get-tuple-element.61), slice={[0:9:1], [0:8:1], [1:1024:2]} | slice | bytes 294912 | tf_op jit(solution)/shard_map/slice | solution.py:68
  167.6 2.1 collective-permute-start.7
  171.8 5.7 %slice.934 = f32[9,8,512]{2,1,0:T(8,128)S(1)} slice(f32[9,8,1024]{2,1,0:T(8,128)S(1)} %fusion.36), slice={[0:9:1], [0:8:1], [0:1024:2]} | slice | bytes 294912 | tf_op jit(solution)/shard_map/slice | solution.py:68
  177.4 5.7 %slice.935 = f32[9,8,512]{2,1,0:T(8,128)S(1)} slice(f32[9,8,1024]{2,1,0:T(8,128)S(1)} %fusion.36), slice={[0:9:1], [0:8:1], [1:1024:2]} | slice | bytes 294912 | tf_op jit(solution)/shard_map/slice | solution.py:68
  184.6 6.7 %collective-permute-done.8 = f32[9,1,512]{2,1,0:T(1,128)S(1)} collective-permute-done((f32[9,1,512]{2,1,0:T(1,128)S(1)}, f32[9,1,512]{2,1,0:T(1,128)S(1)}, u32[]{:S(2)}, u32[]{:S(2)}) %collective-permute-start.8) | collective-permute-done | bytes 18464 | tf_op jit(solution)/shard_map/ppermute | solution.py:20
  191.4 2.5 collective-permute-start.9
  196.6 6.3 %collective-permute-done.10 = f32[9,1,512]{2,1,0:T(1,128)S(1)} collective-permute-done((f32[9,1,512]{2,1,0:T(1,128)S(1)}, f32[9,1,512]{2,1,0:T(1,128)S(1)}, u32[]{:S(2)}, u32[]{:S(2)}) %collective-permute-start.10) | collective-permute-done | bytes 18464 | tf_op jit(solution)/shard_map/ppermute | solution.py:20
  205.7 2.1 collective-permute-start.11
  213.4 6.8 %collective-permute-done.12 = f32[9,1,256]{2,1,0:T(1,128)S(1)} collective-permute-done((f32[9,1,256]{2,1,0:T(1,128)S(1)}, f32[9,1,256]{2,1,0:T(1,128)S(1)}, u32[]{:S(2)}, u32[]{:S(2)}) %collective-permute-start.12) | collective-permute-done | bytes 9248 | tf_op jit(solution)/shard_map/ppermute | solution.py:20
  220.2 2.1 collective-permute-start.13
  224.1 6.9 %collective-permute-done.14 = f32[9,1,256]{2,1,0:T(1,128)S(1)} collective-permute-done((f32[9,1,256]{2,1,0:T(1,128)S(1)}, f32[9,1,256]{2,1,0:T(1,128)S(1)}, u32[]{:S(2)}, u32[]{:S(2)}) %collective-permute-start.14) | collective-permute-done | bytes 9248 | tf_op jit(solution)/shard_map/ppermute | solution.py:20
  232.3 2.3 collective-permute-start.15
  238.3 6.8 %collective-permute-done.16 = f32[9,1,128]{2,1,0:T(1,128)S(1)} collective-permute-done((f32[9,1,128]{2,1,0:T(1,128)S(1)}, f32[9,1,128]{2,1,0:T(1,128)S(1)}, u32[]{:S(2)}, u32[]{:S(2)}) %collective-permute-start.16) | collective-permute-done | bytes 4640 | tf_op jit(solution)/shard_map/ppermute | solution.py:20
  245.1 2.1 collective-permute-start.17
  248.9 6.9 %collective-permute-done.18 = f32[9,1,128]{2,1,0:T(1,128)S(1)} collective-permute-done((f32[9,1,128]{2,1,0:T(1,128)S(1)}, f32[9,1,128]{2,1,0:T(1,128)S(1)}, u32[]{:S(2)}, u32[]{:S(2)}) %collective-permute-start.18) | collective-permute-done | bytes 4640 | tf_op jit(solution)/shard_map/ppermute | solution.py:20
  261.7 24.1 %all-reduce.6 = (f32[8,3,2,128]{3,2,0,1:T(2,128)S(1)}, f32[8,3,1,64]{3,1,2,0:T(4,128)S(1)}, f32[8,1,64]{2,1,0:T(1,128)S(1)}) all-reduce(f32[8,3,2,128]{3,2,0,1:T(2,128)S(1)} %slice_multiply_fusion.6, f32[8,3,1,64]{3,1,2,0:T(4,128)S(1)} %slice_multiply_fusion.10, ...), channel_id=4, replica_groups=mesh['mem'=8,'tile'=32] {'mem'}, use_global_device_ids=true, to_apply=%region_2.3.clone | all-reduce | flops 8192 | bytes 65536
  295.2 5.4 %collective-permute-start.20 = (f32[1,1,128]{2,1,0:T(1,128)S(1)}, f32[1,1,128]{2,1,0:T(1,128)S(1)}, u32[]{:S(2)}, u32[]{:S(2)}) collective-permute-start(f32[1,1,128]{2,1,0:T(1,128)S(1)} %mul.2459), channel_id=1, source_target_pairs={{0,1},{1,2},{2,3},{3,4},{4,5},{5,6},{6,7},{7,8},{8,9},{9,10},{10,1... | collective-permute-start | bytes 1544 | tf_op jit(solution)/shard_map/ppermute | solution.py:20
  301.9 7.1 %collective-permute-done.21 = f32[1,1,128]{2,1,0:T(1,128)S(1)} collective-permute-done((f32[1,1,128]{2,1,0:T(1,128)S(1)}, f32[1,1,128]{2,1,0:T(1,128)S(1)}, u32[]{:S(2)}, u32[]{:S(2)}) %collective-permute-start.21) | collective-permute-done | bytes 544 | tf_op jit(solution)/shard_map/ppermute | solution.py:20
  312.6 6.9 %collective-permute-done.23 = f32[1,1,128]{2,1,0:T(1,128)S(1)} collective-permute-done((f32[1,1,128]{2,1,0:T(1,128)S(1)}, f32[1,1,128]{2,1,0:T(1,128)S(1)}, u32[]{:S(2)}, u32[]{:S(2)}) %collective-permute-start.23) | collective-permute-done | bytes 544 | tf_op jit(solution)/shard_map/ppermute | solution.py:20
  320.8 2.1 collective-permute-start.24
  325.2 6.2 %collective-permute-done.25 = f32[1,1,256]{2,1,0:T(1,128)S(1)} collective-permute-done((f32[1,1,256]{2,1,0:T(1,128)S(1)}, f32[1,1,256]{2,1,0:T(1,128)S(1)}, u32[]{:S(2)}, u32[]{:S(2)}) %collective-permute-start.25) | collective-permute-done | bytes 1056 | tf_op jit(solution)/shard_map/ppermute | solution.py:20
  331.4 2.3 collective-permute-start.26
  335.7 6.6 %collective-permute-done.27 = f32[1,1,256]{2,1,0:T(1,128)S(1)} collective-permute-done((f32[1,1,256]{2,1,0:T(1,128)S(1)}, f32[1,1,256]{2,1,0:T(1,128)S(1)}, u32[]{:S(2)}, u32[]{:S(2)}) %collective-permute-start.27) | collective-permute-done | bytes 1056 | tf_op jit(solution)/shard_map/ppermute | solution.py:20
  342.4 54.5 %all-reduce.10.cloned.1.call-done = (f32[8,3,16,1024]{3,2,0,1:T(8,128)}, f32[8,3,8,512]{3,2,0,1:T(8,128)}, f32[8,3,4,256]{3,2,0,1:T(4,128)}) async-done(((f32[8,3,16,1024]{3,2,0,1:T(8,128)}, f32[8,3,8,512]{3,2,0,1:T(8,128)}, f32[8,3,4,256]{3,2,0,1:T(4,128)}), (f32[8,3,16,1024]{3,2,0,1:T(8,128)}, f32[8,3,8,512]{3,2,0,1:T(8,128)}, f32[8,3,4,256]{3,2,0,1:T(4,128)})) %all-reduce.10.cloned.1.call-update) | async-done | bytes 2064400
  403.2 2.8 collective-permute-start.28
  407.8 6.8 %collective-permute-done.29 = f32[1,1,512]{2,1,0:T(1,128)S(1)} collective-permute-done((f32[1,1,512]{2,1,0:T(1,128)S(1)}, f32[1,1,512]{2,1,0:T(1,128)S(1)}, u32[]{:S(2)}, u32[]{:S(2)}) %collective-permute-start.29) | collective-permute-done | bytes 2080 | tf_op jit(solution)/shard_map/ppermute | solution.py:20
  418.4 6.9 %collective-permute-done.31 = f32[1,1,512]{2,1,0:T(1,128)S(1)} collective-permute-done((f32[1,1,512]{2,1,0:T(1,128)S(1)}, f32[1,1,512]{2,1,0:T(1,128)S(1)}, u32[]{:S(2)}, u32[]{:S(2)}) %collective-permute-start.31) | collective-permute-done | bytes 2080 | tf_op jit(solution)/shard_map/ppermute | solution.py:20
  426.9 2.1 collective-permute-start.32
  430.7 6.9 %collective-permute-done.33 = f32[1,1,1024]{2,1,0:T(1,128)S(1)} collective-permute-done((f32[1,1,1024]{2,1,0:T(1,128)S(1)}, f32[1,1,1024]{2,1,0:T(1,128)S(1)}, u32[]{:S(2)}, u32[]{:S(2)}) %collective-permute-start.33) | collective-permute-done | bytes 4128 | tf_op jit(solution)/shard_map/ppermute | solution.py:20
  441.5 6.9 %collective-permute-done.35 = f32[1,1,1024]{2,1,0:T(1,128)S(1)} collective-permute-done((f32[1,1,1024]{2,1,0:T(1,128)S(1)}, f32[1,1,1024]{2,1,0:T(1,128)S(1)}, u32[]{:S(2)}, u32[]{:S(2)}) %collective-permute-start.35) | collective-permute-done | bytes 4128 | tf_op jit(solution)/shard_map/ppermute | solution.py:20
  451.4 2.3 collective-permute-start.36
  455.5 6.9 %collective-permute-done.37 = f32[1,1,2048]{2,1,0:T(1,128)S(1)} collective-permute-done((f32[1,1,2048]{2,1,0:T(1,128)S(1)}, f32[1,1,2048]{2,1,0:T(1,128)S(1)}, u32[]{:S(2)}, u32[]{:S(2)}) %collective-permute-start.37) | collective-permute-done | bytes 8224 | tf_op jit(solution)/shard_map/ppermute | solution.py:20
  466.4 6.9 %collective-permute-done.39 = f32[1,1,2048]{2,1,0:T(1,128)S(1)} collective-permute-done((f32[1,1,2048]{2,1,0:T(1,128)S(1)}, f32[1,1,2048]{2,1,0:T(1,128)S(1)}, u32[]{:S(2)}, u32[]{:S(2)}) %collective-permute-start.39) | collective-permute-done | bytes 8224 | tf_op jit(solution)/shard_map/ppermute | solution.py:20
  (452 shorter events, 101.4 us)
Async XLA Ops:
  6.5 1.5 copy-start.6
  6.5 390.4 %all-reduce.10.cloned.1.call-start = ((), (), s32[]{:S(2)}) async-start(), calls=%async_computation | async-start | bytes 4128768
  9.5 8.0 %collective-permute-start = (f32[9,1,2048]{2,1,0:T(1,128)}, f32[9,1,2048]{2,1,0:T(1,128)}, u32[]{:S(2)}, u32[]{:S(2)}) collective-permute-start(f32[9,1,2048]{2,1,0:T(1,128)} %slice.1191), channel_id=1, source_target_pairs={{0,31},{1,0},{2,1},{3,2},{4,3},{5,4},{6,5},{7,6},{8,7},{9,8},{10,9... | collective-permute-start | bytes 221192 | tf_op jit(solution)/shard_map/ppermute | solution.py:20
  13.8 3.7 copy-start.2
  18.8 4.4 collective-permute-start.1
  23.6 8.4 %collective-permute-start.2 = (f32[9,1,2048]{2,1,0:T(1,128)S(1)}, f32[9,1,2048]{2,1,0:T(1,128)}, u32[]{:S(2)}, u32[]{:S(2)}) collective-permute-start(f32[9,1,2048]{2,1,0:T(1,128)S(1)} %slice.1195), channel_id=1, source_target_pairs={{0,31},{1,0},{2,1},{3,2},{4,3},{5,4},{6,5},{7,6},{8,7},{9,8},{10,9... | collective-permute-start | bytes 221192 | tf_op jit(solution)/shard_map/ppermute | solution.py:20
  81.1 4.6 collective-permute-start.3
  87.1 22.9 %copy-start.3 = (f32[9,16,2048]{2,1,0:T(8,128)S(1)}, f32[9,16,2048]{2,1,0:T(8,128)}, u32[]{:S(2)}) copy-start(f32[9,16,2048]{2,1,0:T(8,128)} %fusion.8) | copy-start | bytes 3538948
  134.2 1.2 copy-start.5
  135.3 7.6 %collective-permute-start.4 = (f32[9,1,1024]{2,1,0:T(1,128)}, f32[9,1,1024]{2,1,0:T(1,128)}, u32[]{:S(2)}, u32[]{:S(2)}) collective-permute-start(f32[9,1,1024]{2,1,0:T(1,128)} %slice.1207), channel_id=1, source_target_pairs={{0,31},{1,0},{2,1},{3,2},{4,3},{5,4},{6,5},{7,6},{8,7},{9,8},{10,9... | collective-permute-start | bytes 110600 | tf_op jit(solution)/shard_map/ppermute | solution.py:20
  135.6 10.4 %copy-start = (f32[9,1,16,1024]{3,2,0,1:T(8,128)S(1)}, f32[9,1,16,1024]{3,2,0,1:T(8,128)}, u32[]{:S(2)}) copy-start(f32[9,1,16,1024]{3,2,0,1:T(8,128)} %get-tuple-element.65) | copy-start | bytes 1769476
  135.6 10.3 %copy-start.1 = (f32[9,1,16,1024]{3,2,0,1:T(8,128)S(1)}, f32[9,1,16,1024]{3,2,0,1:T(8,128)}, u32[]{:S(2)}) copy-start(f32[9,1,16,1024]{3,2,0,1:T(8,128)} %get-tuple-element.63) | copy-start | bytes 1769476
  143.8 4.0 collective-permute-start.5
  148.0 7.6 %collective-permute-start.6 = (f32[9,1,1024]{2,1,0:T(1,128)S(1)}, f32[9,1,1024]{2,1,0:T(1,128)S(1)}, u32[]{:S(2)}, u32[]{:S(2)}) collective-permute-start(f32[9,1,1024]{2,1,0:T(1,128)S(1)} %slice.1211), channel_id=1, source_target_pairs={{0,31},{1,0},{2,1},{3,2},{4,3},{5,4},{6,5},{7,6},{8,7},{9,8},{10,9... | collective-permute-start | bytes 110600 | tf_op jit(solution)/shard_map/ppermute | solution.py:20
  167.6 4.0 collective-permute-start.7
  184.1 7.2 %collective-permute-start.8 = (f32[9,1,512]{2,1,0:T(1,128)S(1)}, f32[9,1,512]{2,1,0:T(1,128)S(1)}, u32[]{:S(2)}, u32[]{:S(2)}) collective-permute-start(f32[9,1,512]{2,1,0:T(1,128)S(1)} %slice.1223), channel_id=1, source_target_pairs={{0,31},{1,0},{2,1},{3,2},{4,3},{5,4},{6,5},{7,6},{8,7},{9,8},{10,9... | collective-permute-start | bytes 55304 | tf_op jit(solution)/shard_map/ppermute | solution.py:20
  191.4 4.2 collective-permute-start.9
  195.7 7.2 %collective-permute-start.10 = (f32[9,1,512]{2,1,0:T(1,128)S(1)}, f32[9,1,512]{2,1,0:T(1,128)S(1)}, u32[]{:S(2)}, u32[]{:S(2)}) collective-permute-start(f32[9,1,512]{2,1,0:T(1,128)S(1)} %slice.1227), channel_id=1, source_target_pairs={{0,31},{1,0},{2,1},{3,2},{4,3},{5,4},{6,5},{7,6},{8,7},{9,8},{10,9... | collective-permute-start | bytes 55304 | tf_op jit(solution)/shard_map/ppermute | solution.py:20
  205.7 3.8 collective-permute-start.11
  213.1 7.1 %collective-permute-start.12 = (f32[9,1,256]{2,1,0:T(1,128)S(1)}, f32[9,1,256]{2,1,0:T(1,128)S(1)}, u32[]{:S(2)}, u32[]{:S(2)}) collective-permute-start(f32[9,1,256]{2,1,0:T(1,128)S(1)} %get-tuple-element.118), channel_id=1, source_target_pairs={{0,31},{1,0},{2,1},{3,2},{4,3},{5,4},{6,5},{7,6},{8,7},{9,8},{10,9... | collective-permute-start | bytes 27656 | tf_op jit(solution)/shard_map/ppermute | solution.py:20
  220.2 3.7 collective-permute-start.13
  224.0 7.1 %collective-permute-start.14 = (f32[9,1,256]{2,1,0:T(1,128)S(1)}, f32[9,1,256]{2,1,0:T(1,128)S(1)}, u32[]{:S(2)}, u32[]{:S(2)}) collective-permute-start(f32[9,1,256]{2,1,0:T(1,128)S(1)} %get-tuple-element.114), channel_id=1, source_target_pairs={{0,31},{1,0},{2,1},{3,2},{4,3},{5,4},{6,5},{7,6},{8,7},{9,8},{10,9... | collective-permute-start | bytes 27656 | tf_op jit(solution)/shard_map/ppermute | solution.py:20
  232.3 3.9 collective-permute-start.15
  238.1 7.0 %collective-permute-start.16 = (f32[9,1,128]{2,1,0:T(1,128)S(1)}, f32[9,1,128]{2,1,0:T(1,128)S(1)}, u32[]{:S(2)}, u32[]{:S(2)}) collective-permute-start(f32[9,1,128]{2,1,0:T(1,128)S(1)} %slice.1254), channel_id=1, source_target_pairs={{0,31},{1,0},{2,1},{3,2},{4,3},{5,4},{6,5},{7,6},{8,7},{9,8},{10,9... | collective-permute-start | bytes 13832 | tf_op jit(solution)/shard_map/ppermute | solution.py:20
  245.1 3.7 collective-permute-start.17
  248.8 7.0 %collective-permute-start.18 = (f32[9,1,128]{2,1,0:T(1,128)S(1)}, f32[9,1,128]{2,1,0:T(1,128)S(1)}, u32[]{:S(2)}, u32[]{:S(2)}) collective-permute-start(f32[9,1,128]{2,1,0:T(1,128)S(1)} %multiply_add_fusion.1), channel_id=1, source_target_pairs={{0,31},{1,0},{2,1},{3,2},{4,3},{5,4},{6,5},{7,6},{8,7},{9,8},{10,9... | collective-permute-start | bytes 13832 | tf_op jit(solution)/shard_map/ppermute | solution.py:20
  256.9 3.6 collective-permute-start.19
  295.2 6.7 %collective-permute-start.20 = (f32[1,1,128]{2,1,0:T(1,128)S(1)}, f32[1,1,128]{2,1,0:T(1,128)S(1)}, u32[]{:S(2)}, u32[]{:S(2)}) collective-permute-start(f32[1,1,128]{2,1,0:T(1,128)S(1)} %mul.2459), channel_id=1, source_target_pairs={{0,1},{1,2},{2,3},{3,4},{4,5},{5,6},{6,7},{7,8},{8,9},{9,10},{10,1... | collective-permute-start | bytes 1544 | tf_op jit(solution)/shard_map/ppermute | solution.py:20
  301.9 7.1 %collective-permute-start.21 = (f32[1,1,128]{2,1,0:T(1,128)S(1)}, f32[1,1,128]{2,1,0:T(1,128)S(1)}, u32[]{:S(2)}, u32[]{:S(2)}) collective-permute-start(f32[1,1,128]{2,1,0:T(1,128)S(1)} %multiply_subtract_fusion.2), channel_id=1, source_target_pairs={{0,31},{1,0},{2,1},{3,2},{4,3},{5,4},{6,5},{7,6},{8,7},{9,8},{10,9... | collective-permute-start | bytes 1544 | tf_op jit(solution)/shard_map/ppermute | solution.py:20
  309.0 3.5 collective-permute-start.22
  312.6 6.9 %collective-permute-start.23 = (f32[1,1,128]{2,1,0:T(1,128)S(1)}, f32[1,1,128]{2,1,0:T(1,128)S(1)}, u32[]{:S(2)}, u32[]{:S(2)}) collective-permute-start(f32[1,1,128]{2,1,0:T(1,128)S(1)} %multiply_subtract_fusion), channel_id=1, source_target_pairs={{0,31},{1,0},{2,1},{3,2},{4,3},{5,4},{6,5},{7,6},{8,7},{9,8},{10,9... | collective-permute-start | bytes 1544 | tf_op jit(solution)/shard_map/ppermute | solution.py:20
  320.8 3.6 collective-permute-start.24
  324.4 7.0 %collective-permute-start.25 = (f32[1,1,256]{2,1,0:T(1,128)S(1)}, f32[1,1,256]{2,1,0:T(1,128)S(1)}, u32[]{:S(2)}, u32[]{:S(2)}) collective-permute-start(f32[1,1,256]{2,1,0:T(1,128)S(1)} %get-tuple-element.187), channel_id=1, source_target_pairs={{0,31},{1,0},{2,1},{3,2},{4,3},{5,4},{6,5},{7,6},{8,7},{9,8},{10,9... | collective-permute-start | bytes 3080 | tf_op jit(solution)/shard_map/ppermute | solution.py:20
  325.2 75.7 %copy-start.8 = (f32[3]{0:T(128)S(1)}, f32[3]{0:T(128)}, u32[]{:S(2)}) copy-start(f32[3]{0:T(128)} %get-tuple-element.221) | copy-start | bytes 40
  331.4 3.9 collective-permute-start.26
  335.3 7.0 %collective-permute-start.27 = (f32[1,1,256]{2,1,0:T(1,128)S(1)}, f32[1,1,256]{2,1,0:T(1,128)S(1)}, u32[]{:S(2)}, u32[]{:S(2)}) collective-permute-start(f32[1,1,256]{2,1,0:T(1,128)S(1)} %get-tuple-element.190), channel_id=1, source_target_pairs={{0,31},{1,0},{2,1},{3,2},{4,3},{5,4},{6,5},{7,6},{8,7},{9,8},{10,9... | collective-permute-start | bytes 3080 | tf_op jit(solution)/shard_map/ppermute | solution.py:20
  403.2 4.1 collective-permute-start.28
  407.3 7.2 %collective-permute-start.29 = (f32[1,1,512]{2,1,0:T(1,128)S(1)}, f32[1,1,512]{2,1,0:T(1,128)S(1)}, u32[]{:S(2)}, u32[]{:S(2)}) collective-permute-start(f32[1,1,512]{2,1,0:T(1,128)S(1)} %slice.1326), channel_id=1, source_target_pairs={{0,31},{1,0},{2,1},{3,2},{4,3},{5,4},{6,5},{7,6},{8,7},{9,8},{10,9... | collective-permute-start | bytes 6152 | tf_op jit(solution)/shard_map/ppermute | solution.py:20
  414.6 3.7 collective-permute-start.30
  418.3 7.0 %collective-permute-start.31 = (f32[1,1,512]{2,1,0:T(1,128)S(1)}, f32[1,1,512]{2,1,0:T(1,128)S(1)}, u32[]{:S(2)}, u32[]{:S(2)}) collective-permute-start(f32[1,1,512]{2,1,0:T(1,128)S(1)} %slice.1330), channel_id=1, source_target_pairs={{0,31},{1,0},{2,1},{3,2},{4,3},{5,4},{6,5},{7,6},{8,7},{9,8},{10,9... | collective-permute-start | bytes 6152 | tf_op jit(solution)/shard_map/ppermute | solution.py:20
  426.9 3.7 collective-permute-start.32
  430.6 7.0 %collective-permute-start.33 = (f32[1,1,1024]{2,1,0:T(1,128)S(1)}, f32[1,1,1024]{2,1,0:T(1,128)S(1)}, u32[]{:S(2)}, u32[]{:S(2)}) collective-permute-start(f32[1,1,1024]{2,1,0:T(1,128)S(1)} %slice.1362), channel_id=1, source_target_pairs={{0,31},{1,0},{2,1},{3,2},{4,3},{5,4},{6,5},{7,6},{8,7},{9,8},{10,9... | collective-permute-start | bytes 12296 | tf_op jit(solution)/shard_map/ppermute | solution.py:20
  437.6 3.7 collective-permute-start.34
  441.4 7.0 %collective-permute-start.35 = (f32[1,1,1024]{2,1,0:T(1,128)S(1)}, f32[1,1,1024]{2,1,0:T(1,128)S(1)}, u32[]{:S(2)}, u32[]{:S(2)}) collective-permute-start(f32[1,1,1024]{2,1,0:T(1,128)S(1)} %slice.1366), channel_id=1, source_target_pairs={{0,31},{1,0},{2,1},{3,2},{4,3},{5,4},{6,5},{7,6},{8,7},{9,8},{10,9... | collective-permute-start | bytes 12296 | tf_op jit(solution)/shard_map/ppermute | solution.py:20
  451.4 3.9 collective-permute-start.36
  455.4 7.0 %collective-permute-start.37 = (f32[1,1,2048]{2,1,0:T(1,128)S(1)}, f32[1,1,2048]{2,1,0:T(1,128)S(1)}, u32[]{:S(2)}, u32[]{:S(2)}) collective-permute-start(f32[1,1,2048]{2,1,0:T(1,128)S(1)} %slice.1398), channel_id=1, source_target_pairs={{0,31},{1,0},{2,1},{3,2},{4,3},{5,4},{6,5},{7,6},{8,7},{9,8},{10,9... | collective-permute-start | bytes 24584 | tf_op jit(solution)/shard_map/ppermute | solution.py:20
  462.5 3.7 collective-permute-start.38
  466.3 7.0 %collective-permute-start.39 = (f32[1,1,2048]{2,1,0:T(1,128)S(1)}, f32[1,1,2048]{2,1,0:T(1,128)S(1)}, u32[]{:S(2)}, u32[]{:S(2)}) collective-permute-start(f32[1,1,2048]{2,1,0:T(1,128)S(1)} %slice.1402), channel_id=1, source_target_pairs={{0,31},{1,0},{2,1},{3,2},{4,3},{5,4},{6,5},{7,6},{8,7},{9,8},{10,9... | collective-permute-start | bytes 24584 | tf_op jit(solution)/shard_map/ppermute | solution.py:20
  (2 other events, 2.0 us)
Sparse Core Ops, SparseCore 0:
  325.3 71.5 all-reduce.9
where the time goes:
time: 486 us; the launch traced here: 482 us
  waiting for transfers between devices  210 us (43%)
  local copies, waits for them, and re-layouts  149 us (31%)
  starting transfers between devices  50.4 us (10%)
  other arithmetic  32.7 us (7%)
  blocking collectives  24.1 us (5%)
  between operations  15.9 us (3%)
    ppermute x40, waiting for transfers between devices, passed_along(): return lax.ppermute(value, axis, pairs)  155 us
    slice x10, local copies, waits for them, and re-layouts, split_columns(): values[..., 0::2]  61.1 us
    slice x10, local copies, waits for them, and re-layouts, split_columns(): values[..., 1::2]  60.2 us
    unnamed x2, waiting for transfers between devices  54.5 us
    ppermute x40, starting transfers between devices, passed_along(): return lax.ppermute(value, axis, pairs)  50.4 us
    unnamed x1, blocking collectives  24.1 us
  transfers between devices with their start and end apart: 41, of which 41 were waited for; matrix products, arithmetic and copies ran while one was open for 4% of the time, Pallas kernels for 0%

commit v1 on v0

v1 whole, which is shorter than its diff:
```python
import functools

import jax
import jax.numpy as jnp
import numpy as np
from jax import lax
from jax.experimental import pallas as pl
from jax.experimental.pallas import tpu as pltpu
from jax.sharding import PartitionSpec as P

f32, bf16 = jnp.float32, jnp.bfloat16
MESH = pl.DeviceIdType.MESH
LIFT = (-1.586134342059924, -0.052980118572961, 0.882911075530934, 0.443506852043971)
KAPPA = 1.149604398860241
NROW, BAND, LEVELS, MEM, TILE = 1024, 32, 8, 8, 32
RANK = (2, 3, 4)


def forward_matrix(n):
    x = np.eye(n)
    e, o = x[0::2], x[1::2]
    after = lambda v: np.roll(v, -1, 0)
    before = lambda v: np.roll(v, 1, 0)
    o = o + LIFT[0] * (e + after(e))
    e = e + LIFT[1] * (before(o) + o)
    o = o + LIFT[2] * (e + after(e))
    e = e + LIFT[3] * (before(o) + o)
    return e * KAPPA, o / KAPPA


def inverse_matrix(n):
    z = np.eye(n)
    e, o = z[: n // 2] / KAPPA, z[n // 2 :] * KAPPA
    after = lambda v: np.roll(v, -1, 0)
    before = lambda v: np.roll(v, 1, 0)
    e = e - LIFT[3] * (before(o) + o)
    o = o - LIFT[2] * (e + after(e))
    e = e - LIFT[1] * (before(o) + o)
    o = o - LIFT[0] * (e + after(e))
    out = np.zeros((n, n))
    out[0::2], out[1::2] = e, o
    return out


def pieces(m):
    hi = np.asarray(m, np.float32).astype(bf16)
    lo = (np.asarray(m, np.float64) - hi.astype(np.float64)).astype(bf16)
    return hi, lo


def three(m):
    hi, lo = pieces(m)
    return np.concatenate([hi, hi, lo], axis=1)


def two(m):
    hi, lo = pieces(m)
    return np.concatenate([hi, lo], axis=1)


def per_field(m, fields, places=None):
    return np.kron(np.eye(fields), m)


def pad_rows(m, rows):
    return np.concatenate([m, np.zeros((rows - m.shape[0], m.shape[1]))], axis=0)


@functools.lru_cache(maxsize=None)
def constants():
    c = {}
    lows, highs, chain = [], [], np.eye(NROW)
    for k in range(5):
        low, high = forward_matrix(NROW >> k)
        lows.append(low @ chain)
        highs.append(high @ chain)
        chain = lows[-1]
    mid = 16

    def block(mat, k, d):
        r = (BAND >> k) // 2
        m = mat[mid * r : (mid + 1) * r, (mid - d) * BAND : (mid - d + 1) * BAND].copy()
        m[np.abs(m) < 1e-13] = 0.0
        return m

    lo2048, hi2048 = forward_matrix(2048)
    bf = np.concatenate([lo2048[512:640, 896:1408], hi2048[512:640, 896:1408]], axis=0).T
    c["bf_hi"], c["bf_lo"] = pieces(bf)
    l128, h128 = forward_matrix(128)
    c["b4_hi"], c["b4_lo"] = pieces(np.concatenate([l128, h128], axis=0).T)
    s2048 = inverse_matrix(2048)
    bi = np.concatenate([s2048[1024:1280, 384:768], s2048[1024:1280, 1024 + 384 : 1024 + 768]], axis=1).T
    c["bi_hi"], c["bi_lo"] = pieces(bi)
    c["i4_hi"], c["i4_lo"] = pieces(inverse_matrix(128).T)

    for k in range(3):
        bl, bh = {}, {}
        for d in (0, 1, -1):
            bl[d], bh[d] = block(lows[k], k, d), block(highs[k], k, d)
        r = RANK[k]
        rows_h = 16 >> k
        place = {}
        for part in ("h", "l"):
            for d in (1, -1):
                full = np.concatenate([bl[d], bh[d]], axis=0) if part == "h" else bh[d]
                u, s, vt = np.linalg.svd(full, full_matrices=False)
                assert s[r:].max(initial=0.0) < 1e-12
                place[part, d] = (u[:, :r] * s[:r], vt[:r])
        for f, tag in ((8, "m"), (1, "i")):
            if k < 2:
                own_h = np.concatenate([per_field(bl[0], f), per_field(bh[0], f)], axis=0)
                own_l = per_field(bh[0], f)
                uh = {d: np.concatenate([per_field(place["h", d][0][:rows_h], f), per_field(place["h", d][0][rows_h:], f)], axis=0) for d in (1, -1)}
                ul = {d: per_field(place["l", d][0], f) for d in (1, -1)}
            else:
                own_h = per_field(np.concatenate([bl[0], bh[0]], axis=0), f)
                top = lambda m: np.concatenate([m, 0 * m], axis=0)
                bot = lambda m: np.concatenate([0 * m, m], axis=0)
                own_l = np.stack([per_field(top(bh[0]), f), per_field(bot(bh[0]), f)])
                uh = {d: per_field(place["h", d][0], f) for d in (1, -1)}
                ul = {d: np.stack([per_field(top(place["l", d][0]), f), per_field(bot(place["l", d][0]), f)]) for d in (1, -1)}
            c[f"a{k}h{tag}"] = three(own_h)
            rows = 8 if f == 1 else 8 * 2 * r
            for d, name in ((1, "n"), (-1, "p")):
                vh, vl = per_field(place["h", d][1], f), per_field(place["l", d][1], f)
                if f == 1:
                    vh, vl = pad_rows(vh, 8), pad_rows(np.concatenate([0 * vh, vl], axis=0), 8)
                c[f"v{k}h{tag}{name}"], c[f"v{k}l{tag}{name}"] = three(vh), three(vl)
            cut = two if f == 8 else three

            def spread(u, at):
                out = []
                for d in (1, -1):
                    m = np.zeros((u[d].shape[0], rows))
                    m[:, at : at + u[d].shape[1]] = u[d]
                    out.append(m)
                return np.concatenate(out, axis=1)

            c[f"u{k}h{tag}"] = cut(spread(uh, 0))
            if k < 2:
                c[f"a{k}l{tag}"] = three(own_l)
                c[f"u{k}l{tag}"] = cut(spread(ul, f * r))
            else:
                for i in range(2):
                    c[f"a{k}l{i}{tag}"] = three(own_l[i])
                    c[f"u{k}l{i}{tag}"] = cut(spread({d: ul[d][i] for d in ul}, f * r))

    def tile34(d):
        z = np.zeros((8, 3 * BAND))
        z[0:1, :BAND], z[1:2, :BAND] = block(lows[4], 4, d), block(highs[4], 4, d)
        z[2:4, BAND : 2 * BAND] = block(lows[3], 3, d)
        z[4:6, BAND : 2 * BAND] = block(highs[3], 3, d)
        z[6:8, 2 * BAND :] = block(highs[3], 3, d)
        return z

    def tiles(z, f):
        return np.concatenate([per_field(z[:, i * BAND : (i + 1) * BAND], f) for i in range(3)], axis=1)

    for f, tag in ((8, "m"), (1, "i")):
        out = [tiles(tile34(d), f) for d in (0, 1, -1, 2, -2)]
        for d in (3, -3, 4):
            z = tile34(d)
            assert np.abs(z[2:]).max() == 0
            m = tiles(z[:2], f)
            out.append(m if f == 8 else pad_rows(m, 8))
        assert np.abs(tile34(-4)).max() == 0 and np.abs(tile34(5)).max() == 0 and np.abs(tile34(-5)).max() == 0
        c[f"w{tag}"] = three(np.concatenate(out, axis=0))
    spread = np.kron(np.eye(8), np.eye(8)[:, :2])
    spread = np.concatenate([spread, np.zeros((64, 8))], axis=1)
    spread = np.concatenate([spread, np.zeros((8, 24))], axis=0)
    spread[64:66, 16:18] = np.eye(2)
    spread = np.concatenate([spread, np.zeros((72, 8))], axis=1)
    c["x34"] = np.concatenate([spread, spread], axis=1).astype(bf16)

    def row_inverse(k, start, stop, rows_out, low_start, low_count, high_slots):
        n = NROW >> k
        m = inverse_matrix(n)
        m[np.abs(m) < 1e-13] = 0.0
        base = mid * (BAND >> k)
        part = m[base + start : base + stop]
        low, high = part[:, : n // 2], part[:, n // 2 :]
        half = base // 2
        out_low = np.zeros((rows_out, low_count))
        out_low[: stop - start] = low[:, half + low_start : half + low_start + low_count]
        assert np.abs(low).sum() - np.abs(out_low).sum() < 1e-9
        out_high = np.zeros((rows_out, len(high_slots)))
        for i, s in enumerate(high_slots):
            if s is not None:
                out_high[: stop - start, i] = high[:, half + s]
        assert np.abs(high).sum() - np.abs(out_high).sum() < 1e-9, k
        return out_low, out_high

    def pick(k, start, stop, rows_out, low_slots, high_slots):
        n = NROW >> k
        m = inverse_matrix(n)
        m[np.abs(m) < 1e-13] = 0.0
        base = mid * (BAND >> k)
        part = m[base + start : base + stop]
        low, high = part[:, : n // 2], part[:, n // 2 :]
        half = base // 2
        out = np.zeros((rows_out, len(low_slots)))
        seen = 0.0
        for i in range(len(low_slots)):
            if low_slots[i] is not None:
                out[: stop - start, i] += low[:, half + low_slots[i]]
            if high_slots[i] is not None:
                out[: stop - start, i] += high[:, half + high_slots[i]]
        want = (np.abs(low).sum() if any(s is not None for s in low_slots) else 0.0) + (
            np.abs(high).sum() if any(s is not None for s in high_slots) else 0.0
        )
        assert abs(want - np.abs(out).sum()) < 1e-9, k
        return out

    none = [None]
    bands = list(range(-3, 5))
    flat = lambda rows: sum(rows, [])
    l4 = flat([[b] + none * 7 for b in bands])
    h4 = flat([none + [b] + none * 6 for b in bands])
    c["s4"] = three(pick(4, -2, 6, 8, l4, h4))
    l3 = flat([none * 2 + [2 * b, 2 * b + 1] + none * 4 for b in bands])
    h3 = flat([none * 4 + [2 * b, 2 * b + 1] + none * 2 for b in bands])
    h3l = flat([none * 6 + [2 * b, 2 * b + 1] for b in bands])
    c["s3h"] = three(pick(3, -2, 8, 16, l3, h3))
    c["s3l"] = three(pick(3, -2, 8, 16, none * 64 + list(range(-2, 6)) + none * 8, h3l + none * 16))
    near = (-1, 0, 1)
    l2 = flat([[4 * b + i for i in range(4)] + none * 4 for b in near]) + none * 8
    h2 = flat([none * 4 + [4 * b + i for i in range(4)] for b in near]) + none * 8
    c["s2h"] = three(pick(2, -2, 12, 16, l2, h2))
    low_ext = [-2 + i if i < 10 else None for i in range(16)]
    ha = flat([[4 * b + i for i in range(4)] + none * 4 for b in near]) + none * 8
    hb = flat([none * 4 + [4 * b + i for i in range(4)] for b in near]) + none * 8
    c["s2l0"] = three(pick(2, -2, 12, 16, none * 32 + low_ext, ha + none * 16))
    c["s2l1"] = three(pick(2, -2, 12, 16, none * 32 + low_ext, hb + none * 16))
    s1 = list(range(8)) + list(range(-4, 0)) + list(range(8, 12))
    c["s1h"] = three(pick(1, -2, 18, 24, s1 + none * 16, none * 16 + s1))
    low_ext = [-2 + i if i < 14 else None for i in range(16)]
    c["s1l"] = three(pick(1, -2, 18, 24, low_ext + none * 16, none * 16 + s1))
    s0 = list(range(16)) + [-2, -1, 16, 17] + none * 4
    c["s0h"] = three(pick(0, 0, 32, 32, s0 + none * 24, none * 24 + s0))
    low_ext = [-2 + i if i < 20 else None for i in range(24)]
    c["s0l"] = three(pick(0, 0, 32, 32, low_ext + none * 24, none * 24 + s0))
    return c


def split(x):
    hi = x.astype(bf16)
    return hi, (x - hi.astype(f32)).astype(bf16)


def dot(a, b):
    return jnp.dot(a, b, preferred_element_type=f32)


def rows(*parts):
    return jnp.concatenate(parts, axis=0)


def lanes(*parts):
    return jnp.concatenate(parts, axis=1)


def left(matrix, x):
    hi, lo = split(x)
    return dot(matrix, rows(hi, lo, hi))


NAMES = tuple(sorted(constants()))


def kernel(*refs):
    members, increment, weights = refs[:3]
    c = dict(zip(NAMES, refs[3 : 3 + len(NAMES)]))
    out = refs[3 + len(NAMES)]
    (t_hi, t_lo, u_hi, u_lo, y0, y1, yc, i0, i1, ic,
     hs0, hs1, hs2, hr0, hr1, hr2, gs0, gs1, gs2, gr0, gr1, gr2, ks, kr, qs, qr,
     e0, e1, ce0, ce1, es0, es1, er0, er1, p0, p1, pc, ss0, ss1, sr0, sr1, syc, srt,
     sem_s, sem_r) = refs[4 + len(NAMES):]
    mem, tile = lax.axis_index("mem"), lax.axis_index("tile")
    ypos, core = lax.div(mem, 2), lax.rem(mem, 2)

    def at_tile(d):
        return (mem, lax.rem(tile + TILE + d, TILE))

    def at_y(j):
        return (lax.rem(ypos + j, 4) * 2 + core, tile)

    partner = (ypos * 2 + 1 - core, tile)
    near = [at_tile(d) for d in (1, -1, 2, -2, 3, -3, 4, -4)] + [partner] + [at_y(j) for j in (1, 2, 3)]
    barrier = pltpu.get_barrier_semaphore()
    for device in near:
        pl.semaphore_signal(barrier, inc=1, device_id=device, device_id_type=MESH)

    sent = []

    def send(src, dst, device):
        n = len(sent)
        copy = pltpu.make_async_remote_copy(
            src_ref=src, dst_ref=dst, send_sem=sem_s.at[n], recv_sem=sem_r.at[n], device_id=device, device_id_type=MESH
        )
        copy.start()
        sent.append(copy)
        return copy

    bf_hi, bf_lo = c["bf_hi"], c["bf_lo"]

    def window(ref, width, j, first, last):
        start = 256 * j - 128
        tiles = [(start // 128 + i) % (width // 128) for i in range(4)]
        groups = []
        for t in tiles:
            if groups and groups[-1][1] == t:
                groups[-1][1] = t + 1
            else:
                groups.append([t, t + 1])
        return lanes(*[ref[first:last, 128 * a : 128 * b] for a, b in groups]) if len(groups) > 1 else ref[first:last, 128 * groups[0][0] : 128 * groups[0][1]]

    def put(hi_ref, lo_ref, first, last, width, j, r):
        hi, lo = split(r)
        half = width // 2
        for ref, v in ((hi_ref, hi), (lo_ref, lo)):
            ref[first:last, 128 * j : 128 * j + 128] = v[:, :128]
            ref[first:last, half + 128 * j : half + 128 * j + 128] = v[:, 128:]

    m_all = members
    inc = increment[...]
    inc_hi, inc_lo = split(inc)
    for j in range(8):
        w = window(m_all, 2048, j, 0, 256)
        put(t_hi, t_lo, 0, 256, 2048, j, dot(w, bf_hi[...]) + dot(w, bf_lo[...]))
    u_hi[...] = inc_hi
    u_lo[...] = inc_lo
    for j in range(8):
        a, b = window(u_hi, 2048, j, 0, 32), window(u_lo, 2048, j, 0, 32)
        put(t_hi, t_lo, 256, 288, 2048, j, dot(a, bf_hi[...]) + dot(b, bf_hi[...]) + dot(a, bf_lo[...]))

    base = [0, 2048, 3072, 3584, 3840]

    def part(k, which, first, last):
        half = 1024 >> k
        s = base[k] + (half if which == "h" else 0)
        hi, lo = t_hi[first:last, s : s + half], t_lo[first:last, s : s + half]
        return rows(hi, lo, hi)

    def halo(k, hs, hr, gs, gr):
        copies = []
        for n, (name, d) in enumerate((("n", 1), ("p", -1))):
            h = rows(dot(c[f"v{k}hm{name}"][...], part(k, "h", 0, 256)), dot(c[f"v{k}lm{name}"][...], part(k, "l", 0, 256)))
            hs[n] = h.astype(bf16)
            if not sent:
                pl.semaphore_wait(barrier, len(near))
            copies.append(send(hs.at[n], hr.at[n], at_tile(d)))
            gs[n] = dot(c[f"v{k}hi{name}"][...], part(k, "h", 256, 288)) + dot(c[f"v{k}li{name}"][...], part(k, "l", 256, 288))
            copies.append(send(gs.at[n], gr.at[n], at_tile(d)))
        return copies

    halos = [halo(0, hs0, hr0, gs0, gr0)]
    for k in range(1, 5):
        width = 2048 >> k
        src = base[k - 1]
        if k < 4:
            for j in range(max(width // 256, 1)):
                a = window(t_hi.at[:, src : src + width], width, j, 0, 288)
                b = window(t_lo.at[:, src : src + width], width, j, 0, 288)
                r = dot(a, bf_hi[...]) + dot(b, bf_hi[...]) + dot(a, bf_lo[...])
                put(t_hi.at[:, base[k] : base[k] + width], t_lo.at[:, base[k] : base[k] + width], 0, 288, width, j, r)
        else:
            a, b = t_hi[:, src : src + 128], t_lo[:, src : src + 128]
            r = dot(a, c["b4_hi"][...]) + dot(b, c["b4_hi"][...]) + dot(a, c["b4_lo"][...])
            hi, lo = split(r)
            t_hi[:, base[4] : base[4] + 128] = hi
            t_lo[:, base[4] : base[4] + 128] = lo
        if k == 1:
            halos.append(halo(1, hs1, hr1, gs1, gr1))
        if k == 2:
            halos.append(halo(2, hs2, hr2, gs2, gr2))

    def stack34(first, last):
        hi = rows(*[t_hi[first:last, s : s + 128] for s in (base[4], base[3] + 128, base[3])])
        lo = rows(*[t_lo[first:last, s : s + 128] for s in (base[4], base[3] + 128, base[3])])
        return rows(hi, lo, hi)

    wm = dot(c["wm"][...], stack34(0, 256))
    wi = dot(c["wi"][...], stack34(256, 288))
    yc[:, 384:] = wm[0:64]
    ic[:, 384:] = wi[0:8]
    far = []
    for n, d in enumerate((1, -1, 2, -2)):
        ks[n] = rows(wm[64 + 64 * n : 128 + 64 * n], wi[8 + 8 * n : 16 + 8 * n])
        far.append(send(ks.at[n], kr.at[n], at_tile(d)))
    for n, d in enumerate((3, -3, 4)):
        qs[n] = rows(wm[320 + 16 * n : 336 + 16 * n], wi[40 + 8 * n : 48 + 8 * n])
        far.append(send(qs.at[n], qr.at[n], at_tile(d)))

    y = dot(c["a0hm"][...], part(0, "h", 0, 256))
    y0[:, 0:1024], y0[:, 1024:2048] = y[:128], y[128:]
    y0[:, 2048:] = dot(c["a0lm"][...], part(0, "l", 0, 256))
    y = dot(c["a0hi"][...], part(0, "h", 256, 288))
    i0[:, 0:1024], i0[:, 1024:2048] = y[:16], y[16:]
    i0[:, 2048:] = dot(c["a0li"][...], part(0, "l", 256, 288))
    y = dot(c["a1hm"][...], part(1, "h", 0, 256))
    y1[:, 0:512], y1[:, 512:1024] = y[:64], y[64:]
    y1[:, 1024:] = dot(c["a1lm"][...], part(1, "l", 0, 256))
    y = dot(c["a1hi"][...], part(1, "h", 256, 288))
    i1[:, 0:512], i1[:, 512:1024] = y[:8], y[8:]
    i1[:, 1024:] = dot(c["a1li"][...], part(1, "l", 256, 288))
    for ref, tag, first, last in ((yc, "m", 0, 256), (ic, "i", 256, 288)):
        ref[:, 0:256] = dot(c[f"a2h{tag}"][...], part(2, "h", first, last))
        p = part(2, "l", first, last)
        ref[:, 256:384] = dot(c[f"a2l0{tag}"][...], p[:, :128]) + dot(c[f"a2l1{tag}"][...], p[:, 128:])

    def got(ref):
        a, b = ref[0], ref[1]
        return rows(a, b, a, b)

    def got_inc(ref):
        hi, lo = split(rows(ref[0], ref[1]))
        return rows(hi, lo, hi)

    for copy in halos[0]:
        copy.wait_recv()
    g = got(hr0)
    q = dot(c["u0hm"][...], g)
    v = y0[:, 0:1024] + q[:128]
    e0[:, :, :, 0:1024] = (v * v).reshape(4, 2, 16, 1024)
    v = y0[:, 1024:2048] + q[128:]
    e0[:, :, :, 1024:2048] = (v * v).reshape(4, 2, 16, 1024)
    v = y0[:, 2048:] + dot(c["u0lm"][...], g)
    e0[:, :, :, 2048:] = (v * v).reshape(4, 2, 16, 1024)
    pair0 = send(e0.at[:, 1 - core], ce0, partner)

    for copy in halos[1]:
        copy.wait_recv()
    g = got(hr1)
    q = dot(c["u1hm"][...], g)
    v = y1[:, 0:512] + q[:64]
    e1[:, :, :, 0:512] = (v * v).reshape(4, 2, 8, 512)
    v = y1[:, 512:1024] + q[64:]
    e1[:, :, :, 512:1024] = (v * v).reshape(4, 2, 8, 512)
    v = y1[:, 1024:] + dot(c["u1lm"][...], g)
    e1[:, :, :, 1024:1536] = (v * v).reshape(4, 2, 8, 512)
    for copy in halos[2]:
        copy.wait_recv()
    g = got(hr2)
    v = yc[:, 0:256] + dot(c["u2hm"][...], g)
    e1[:, :, :, 1536:1792] = (v * v).reshape(4, 2, 8, 256)
    v = yc[:, 256:384] + dot(c["u2l0m"][...], g[:, :128]) + dot(c["u2l1m"][...], g[:, 128:])
    e1[:, :, :, 1792:1920] = (v * v).reshape(4, 2, 8, 128)
    for copy in far:
        copy.wait_recv()
    hi, lo = split(rows(qr[0] + qr[1] + qr[2], jnp.zeros((8, 128), f32)))
    v34 = kr[0] + kr[1] + kr[2] + kr[3] + dot(c["x34"][...], rows(hi, lo))
    v = yc[:, 384:] + v34[:64]
    e1[:, :, :, 1920:] = (v * v).reshape(4, 2, 8, 128)
    pair1 = send(e1.at[:, 1 - core], ce1, partner)

    g = got_inc(gr0)
    q = dot(c["u0hi"][...], g)
    i0[:, 0:1024] += q[:16]
    i0[:, 1024:2048] += q[16:]
    i0[:, 2048:] += dot(c["u0li"][...], g)
    g = got_inc(gr1)
    q = dot(c["u1hi"][...], g)
    i1[:, 0:512] += q[:8]
    i1[:, 512:1024] += q[8:]
    i1[:, 1024:] += dot(c["u1li"][...], g)
    g = got_inc(gr2)
    ic[:, 0:256] += dot(c["u2hi"][...], g)
    ic[:, 256:384] += dot(c["u2l0i"][...], g[:, :128]) + dot(c["u2l1i"][...], g[:, 128:])
    ic[:, 384:] += v34[64:72]

    pair0.wait_recv()
    over0 = []
    for j in (2, 1, 3):
        q = lax.rem(ypos + j, 4)
        both = e0[q, core] + ce0[q]
        es0[j - 1] = (both * both).astype(bf16)
        over0.append(send(es0.at[j - 1], er0.at[j - 1], at_y(j)))
    pair1.wait_recv()
    over1 = []
    for j in (2, 1, 3):
        q = lax.rem(ypos + j, 4)
        es1[j - 1] = e1[q, core] + ce1[q]
        over1.append(send(es1.at[j - 1], er1.at[j - 1], at_y(j)))
    own0 = e0[ypos, core] + ce0[ypos]
    own1 = e1[ypos, core] + ce1[ypos]

    w = [weights[i] * (1.0 / (MEM - 1)) for i in range(16)]
    for copy in over0:
        copy.wait_recv()
    energy = own0 + jnp.sqrt(er0[0].astype(f32)) + jnp.sqrt(er0[1].astype(f32)) + jnp.sqrt(er0[2].astype(f32))
    p0[:, 0:1024] = w[0] * energy[:, 0:1024] * i0[:, 0:1024]
    p0[:, 1024:2048] = w[2] * energy[:, 1024:2048] * i0[:, 1024:2048]
    p0[:, 2048:] = w[1] * energy[:, 2048:] * i0[:, 2048:]
    ss0[0] = p0[14:16]
    ss0[1] = p0[0:2]
    syn0 = [send(ss0.at[n], sr0.at[n], at_tile(d)) for n, d in enumerate((1, -1))]

    for copy in over1:
        copy.wait_recv()
    energy = own1 + er1[0] + er1[1] + er1[2]
    row = lax.broadcasted_iota(jnp.int32, (8, 128), 0)
    lane = lax.broadcasted_iota(jnp.int32, (8, 128), 1)
    w34 = jnp.where(
        row < 2,
        jnp.where(row == 0, jnp.where(lane < 64, w[15], w[12]), jnp.where(lane < 64, w[13], w[14])),
        jnp.where(row < 4, w[9], jnp.where(row < 6, w[11], w[10])),
    )
    w2 = jnp.where(lax.broadcasted_iota(jnp.int32, (8, 256), 0) < 4, w[6], w[8])
    pc[:, 0:256] = w2 * energy[:, 1536:1792] * ic[:, 0:256]
    pc[:, 256:384] = w[7] * energy[:, 1792:1920] * ic[:, 256:384]
    pc[:, 384:] = w34 * energy[:, 1920:] * ic[:, 384:]
    sync = [send(pc, syc.at[n], at_tile(d)) for n, d in enumerate((1, -1))]
    synt = [send(pc.at[:, 384:], srt.at[n], at_tile(d)) for n, d in enumerate((2, -2, 3, -3, -4))]
    p1[:, 0:512] = w[0 + 3] * energy[:, 0:512] * i1[:, 0:512]
    p1[:, 512:1024] = w[2 + 3] * energy[:, 512:1024] * i1[:, 512:1024]
    p1[:, 1024:] = w[1 + 3] * energy[:, 1024:1536] * i1[:, 1024:]
    ss1[0] = p1[4:8]
    ss1[1] = p1[0:4]
    syn1 = [send(ss1.at[n], sr1.at[n], at_tile(d)) for n, d in enumerate((1, -1))]

    for copy in synt + sync:
        copy.wait_recv()
    t = {-2: srt[0], 2: srt[1], -3: srt[2], 3: srt[3], 4: srt[4], 0: pc[:, 384:], -1: syc[0, :, 384:], 1: syc[1, :, 384:]}
    stack = rows(*[t[b] for b in range(-3, 5)])
    x = left(c["s4"][...], stack)
    hi, lo = split(x)
    ll3 = dot(hi, c["i4_hi"][...]) + dot(lo, c["i4_hi"][...]) + dot(hi, c["i4_lo"][...])
    x = lanes(left(c["s3l"][...], rows(stack, ll3, jnp.zeros((8, 128), f32))), left(c["s3h"][...], stack))

    bi_hi, bi_lo = c["bi_hi"], c["bi_lo"]

    def columns(x):
        half = x.shape[1] // 2
        hi, lo = split(x)
        outs = []
        count = half // 128

        def win(v, j):
            return lanes(*[v[:, s + 128 * ((j + i) % count) : s + 128 * ((j + i) % count) + 128] for s in (0, half) for i in (-1, 0, 1)])

        for j in range(count):
            a, b = win(hi, j), win(lo, j)
            outs.append(dot(a, bi_hi[...]) + dot(b, bi_hi[...]) + dot(a, bi_lo[...]))
        return lanes(*outs) if count > 1 else outs[0]

    ll2 = columns(x)
    z = jnp.zeros((8, 384), f32)
    stack = rows(syc[0, :, 0:384], pc[:, 0:384], syc[1, :, 0:384], z)
    x = lanes(
        left(c["s2l0"][...], rows(stack[:, 256:384], ll2[:, :128])),
        left(c["s2l1"][...], rows(stack[:, 256:384], ll2[:, 128:])),
        left(c["s2h"][...], stack[:, :256]),
    )
    ll1 = columns(x)
    for copy in syn1:
        copy.wait_recv()
    stack = rows(p1[...], sr1[0], sr1[1])
    x = lanes(
        left(c["s1l"][...], rows(ll1, stack[:, 1024:])),
        left(c["s1h"][...], rows(stack[:, 0:512], stack[:, 512:1024])),
    )
    ll0 = columns(x)
    for copy in syn0:
        copy.wait_recv()
    stack = rows(p0[...], sr0[0], sr0[1], jnp.zeros((4, 3072), f32))
    x = lanes(
        left(c["s0l"][...], rows(ll0, stack[:, 2048:])),
        left(c["s0h"][...], rows(stack[:, 0:1024], stack[:, 1024:2048])),
    )
    out[...] = columns(x)
    for copy in sent:
        copy.wait_send()


def local(members, increment, weights):
    c = constants()
    vmem = pl.BlockSpec(memory_space=pltpu.VMEM)
    v = pltpu.VMEM
    scratch = [
        v((288, 3968), bf16), v((288, 3968), bf16), v((32, 2048), bf16), v((32, 2048), bf16),
        v((128, 3072), f32), v((64, 1536), f32), v((64, 512), f32),
        v((16, 3072), f32), v((8, 1536), f32), v((8, 512), f32),
        v((2, 32, 1024), bf16), v((2, 48, 512), bf16), v((2, 64, 256), bf16),
        v((2, 32, 1024), bf16), v((2, 48, 512), bf16), v((2, 64, 256), bf16),
        v((2, 8, 1024), f32), v((2, 8, 512), f32), v((2, 8, 256), f32),
        v((2, 8, 1024), f32), v((2, 8, 512), f32), v((2, 8, 256), f32),
        v((4, 72, 128), f32), v((4, 72, 128), f32), v((3, 24, 128), f32), v((3, 24, 128), f32),
        v((4, 2, 16, 3072), f32), v((4, 2, 8, 2048), f32), v((4, 16, 3072), f32), v((4, 8, 2048), f32),
        v((3, 16, 3072), bf16), v((3, 8, 2048), f32), v((3, 16, 3072), bf16), v((3, 8, 2048), f32),
        v((16, 3072), f32), v((8, 1536), f32), v((8, 512), f32),
        v((2, 2, 3072), f32), v((2, 4, 1536), f32), v((2, 2, 3072), f32), v((2, 4, 1536), f32),
        v((2, 8, 512), f32), v((5, 8, 128), f32),
        pltpu.SemaphoreType.DMA((40,)), pltpu.SemaphoreType.DMA((40,)),
    ]
    result = pl.pallas_call(
        kernel,
        out_shape=jax.ShapeDtypeStruct((BAND, 2048), f32),
        in_specs=[vmem, vmem, pl.BlockSpec(memory_space=pltpu.SMEM)] + [vmem] * len(NAMES),
        out_specs=vmem,
        scratch_shapes=scratch,
        compiler_params=pltpu.CompilerParams(collective_id=0, has_side_effects=True, vmem_limit_bytes=56 * 2**20),
    )(members.reshape(256, 2048), increment.reshape(BAND, 2048), weights, *[jnp.asarray(c[n]) for n in NAMES])
    return result.reshape(1, BAND, 2048)


def solution(mesh):
    return jax.shard_map(
        local,
        mesh=mesh,
        in_specs=(P("mem", None, "tile", None), P("mem", "tile", None), P()),
        out_specs=P("mem", "tile", None),
        check_vma=False,
    )
```

time: 486 us -> 43.3 us (0.09)
  the two profiles are of different devices: /device:TPU:102 before, /device:TPU:1 now
where the time goes in v1:
time: 43.3 us; the launch traced here: 42.7 us
  Pallas kernels  41 us (95%)
  local copies, waits for them, and re-layouts  1.67 us (4%)
    pallas_call x1, Pallas kernels, local(): pl.pallas_call(kernel, out_shape=jax.ShapeDtypeStruct((BAND, 2048), f32),...  41 us
    unnamed x1, local copies, waits for them, and re-layouts  1.67 us

profile of v1, /device:TPU:1, one launch (start us, length us, event | category | flops | bytes accessed | tf_op | source)
XLA Modules:
  0.0 42.7 jit_solution(10421177397723288974)
XLA Ops:
  0.0 41.0 %shard_map.694 = f32[32,2048]{1,0:T(8,128)} custom-call(bf16[256,2048]{1,0:T(8,128)(2,1)} %bitcast.4, f32[32,2048]{1,0:T(8,128)} %bitcast.5, f32[16]{0:T(128)} %refs_2_.1, bf16[32,96]{1,0:T(8,128)(2,1)} %constant.146.clone.refs_3_, bf16[256,768]{1,0:T(8,128)(2,1)} %constant.147.clone.refs_4_, bf16[16,96]{1,0:T(8,128)(2,1)} %constant.148.clone.refs_5_, ...), custom_call_target="tpu_custom_call" | custom-call | tf_op jit(solution)/shard_map/pallas_call | solution.py:595
  41.0 1.7 %copy.78 = f32[1,32,2048]{2,1,0:T(8,128)} copy(f32[1,32,2048]{2,1,0:T(8,128)} %bitcast.3) | data formatting | bytes 524288

commit v2 on v1

v2 whole, which is shorter than its diff:
```python
import functools

import jax
import jax.numpy as jnp
import numpy as np
from jax import lax
from jax.experimental import pallas as pl
from jax.experimental.pallas import tpu as pltpu
from jax.sharding import PartitionSpec as P

f32, bf16 = jnp.float32, jnp.bfloat16
MESH = pl.DeviceIdType.MESH
LIFT = (-1.586134342059924, -0.052980118572961, 0.882911075530934, 0.443506852043971)
KAPPA = 1.149604398860241
NROW, BAND, LEVELS, MEM, TILE = 1024, 32, 8, 8, 32
RANK = (2, 3, 4)


def forward_matrix(n):
    x = np.eye(n)
    e, o = x[0::2], x[1::2]
    after = lambda v: np.roll(v, -1, 0)
    before = lambda v: np.roll(v, 1, 0)
    o = o + LIFT[0] * (e + after(e))
    e = e + LIFT[1] * (before(o) + o)
    o = o + LIFT[2] * (e + after(e))
    e = e + LIFT[3] * (before(o) + o)
    return e * KAPPA, o / KAPPA


def inverse_matrix(n):
    z = np.eye(n)
    e, o = z[: n // 2] / KAPPA, z[n // 2 :] * KAPPA
    after = lambda v: np.roll(v, -1, 0)
    before = lambda v: np.roll(v, 1, 0)
    e = e - LIFT[3] * (before(o) + o)
    o = o - LIFT[2] * (e + after(e))
    e = e - LIFT[1] * (before(o) + o)
    o = o - LIFT[0] * (e + after(e))
    out = np.zeros((n, n))
    out[0::2], out[1::2] = e, o
    return out


def pieces(m):
    hi = np.asarray(m, np.float32).astype(bf16)
    lo = (np.asarray(m, np.float64) - hi.astype(np.float64)).astype(bf16)
    return hi, lo


def three(m):
    hi, lo = pieces(m)
    return np.concatenate([hi, hi, lo], axis=1)


def two(m):
    hi, lo = pieces(m)
    return np.concatenate([hi, lo], axis=1)


def per_field(m, fields, places=None):
    return np.kron(np.eye(fields), m)


def pad_rows(m, rows):
    return np.concatenate([m, np.zeros((rows - m.shape[0], m.shape[1]))], axis=0)


@functools.lru_cache(maxsize=None)
def constants():
    c = {}
    lows, highs, chain = [], [], np.eye(NROW)
    for k in range(5):
        low, high = forward_matrix(NROW >> k)
        lows.append(low @ chain)
        highs.append(high @ chain)
        chain = lows[-1]
    mid = 16

    def block(mat, k, d):
        r = (BAND >> k) // 2
        m = mat[mid * r : (mid + 1) * r, (mid - d) * BAND : (mid - d + 1) * BAND].copy()
        m[np.abs(m) < 1e-13] = 0.0
        return m

    def halves(m):
        return np.concatenate(pieces(m), axis=1)

    lo2048, hi2048 = forward_matrix(2048)
    bf = np.concatenate([lo2048[512:640, 896:1408], hi2048[512:640, 896:1408]], axis=0).T
    c["bf"] = np.concatenate(pieces(bf), axis=0)
    l128, h128 = forward_matrix(128)
    c["b4"] = np.concatenate(pieces(np.concatenate([l128, h128], axis=0).T), axis=0)
    s2048 = inverse_matrix(2048)
    bi = np.concatenate([s2048[1024:1280, 384:768], s2048[1024:1280, 1024 + 384 : 1024 + 768]], axis=1).T
    c["bi"] = np.concatenate(pieces(bi), axis=0)
    c["i4"] = np.concatenate(pieces(inverse_matrix(128).T), axis=0)

    inner, edge = list(range(4, 12)), [0, 1, 2, 3, 12, 13, 14, 15]
    for k in range(3):
        bl = {d: block(lows[k], k, d) for d in (0, 1, -1)}
        bh = {d: block(highs[k], k, d) for d in (0, 1, -1)}
        r = RANK[k]
        rows_h = 16 >> k
        place = {}
        for part in ("h", "l"):
            for d in (1, -1):
                full = np.concatenate([bl[d], bh[d]], axis=0) if part == "h" else bh[d]
                u, s, vt = np.linalg.svd(full, full_matrices=False)
                assert s[r:].max(initial=0.0) < 1e-12
                keep = s[:r] > 1e-12
                place[part, d] = (u[:, :r] * s[:r] * keep, vt[:r] * keep[:, None])
        top = lambda m: np.concatenate([m, 0 * m], axis=0)
        bot = lambda m: np.concatenate([0 * m, m], axis=0)
        for f, tag in ((8, "m"), (1, "i")):
            width = 8 * 2 * r if f == 8 else (4, 8, 8)[k]

            def sent(part):
                out = []
                for d in (1, -1):
                    v = place[part, d][1]
                    if f == 8:
                        out.append(per_field(v, f))
                    else:
                        out.append(pad_rows(np.concatenate([np.zeros((r if part == "l" else 0, BAND)), v], axis=0), 8))
                return out

            def spread(u, at):
                out = []
                for d in (1, -1):
                    m = np.zeros((u[d].shape[0], width))
                    m[:, at : at + u[d].shape[1]] = u[d]
                    out.append(m)
                m = np.concatenate(out, axis=1)
                if f == 1 and m.shape[1] < 16:
                    m = np.concatenate([m, np.zeros((m.shape[0], 16 - m.shape[1]))], axis=1)
                return m

            at_l = f * r
            if k == 0:
                own_h = [per_field(m[rows_], f) for rows_ in (inner, edge) for m in (bl[0], bh[0])]
                own_l = [per_field(bh[0][rows_], f) for rows_ in (inner, edge)]
                uh = {d: np.concatenate([per_field(place["h", d][0][:16][edge], f), per_field(place["h", d][0][16:][edge], f)], axis=0) for d in (1, -1)}
                ul = {d: per_field(place["l", d][0][edge], f) for d in (1, -1)}
                full_h = {d: place["h", d][0] for d in (1, -1)}
                assert all(np.abs(full_h[d][:16][inner]).max() < 1e-12 and np.abs(full_h[d][16:][inner]).max() < 1e-12 for d in full_h)
            elif k == 1:
                own_h = [per_field(bl[0], f), per_field(bh[0], f)]
                own_l = [per_field(bh[0], f)]
                uh = {d: np.concatenate([per_field(place["h", d][0][:rows_h], f), per_field(place["h", d][0][rows_h:], f)], axis=0) for d in (1, -1)}
                ul = {d: per_field(place["l", d][0], f) for d in (1, -1)}
            else:
                own_h = [per_field(np.concatenate([bl[0], bh[0]], axis=0), f)]
                own_l = [per_field(top(bh[0]), f), per_field(bot(bh[0]), f)]
                uh = {d: per_field(place["h", d][0], f) for d in (1, -1)}
                ul = {d: np.concatenate([per_field(top(place["l", d][0]), f), per_field(bot(place["l", d][0]), f)], axis=0) for d in (1, -1)}
            if k == 0 and f == 8:
                for part in ("h", "l"):
                    n, p = place[part, 1][1], place[part, -1][1]
                    assert np.abs(n[:, :24]).max() < 1e-12 and np.abs(p[:, 8:]).max() < 1e-12
                    n, p = per_field(n[:, 24:], f), per_field(p[:, :8], f)
                    z = np.zeros_like(n)
                    c[f"v0{part}"] = halves(np.concatenate([np.concatenate([n, z], axis=1), np.concatenate([z, p], axis=1)], axis=0))
                c["a0h"], c["a0l"] = halves(np.concatenate(own_h, axis=0)), halves(np.concatenate(own_l, axis=0))
            else:
                cut = halves if f == 8 else three
                c[f"a{k}h" + tag * (f == 1)] = cut(np.concatenate(own_h + sent("h"), axis=0))
                c[f"a{k}l" + tag * (f == 1)] = cut(np.concatenate(own_l + sent("l"), axis=0))
            cut = two if f == 8 else three
            c[f"u{k}h" + tag * (f == 1)] = cut(spread(uh, 0))
            c[f"u{k}l" + tag * (f == 1)] = cut(spread(ul, at_l))

    def tile34(d):
        z = np.zeros((8, 3 * BAND))
        z[0:1, :BAND], z[1:2, :BAND] = block(lows[4], 4, d), block(highs[4], 4, d)
        z[2:4, BAND : 2 * BAND] = block(lows[3], 3, d)
        z[4:6, BAND : 2 * BAND] = block(highs[3], 3, d)
        z[6:8, 2 * BAND :] = block(highs[3], 3, d)
        return z

    def tiles(z, f):
        return np.concatenate([per_field(z[:, i * BAND : (i + 1) * BAND], f) for i in range(3)], axis=1)

    for f, tag in ((8, "m"), (1, "i")):
        out = [tiles(tile34(d), f) for d in (0, 1, -1, 2, -2)]
        for d in (3, -3, 4):
            z = tile34(d)
            assert np.abs(z[2:]).max() == 0
            m = tiles(z[:2], f)
            out.append(m if f == 8 else pad_rows(m, 8))
        assert np.abs(tile34(-4)).max() == 0 and np.abs(tile34(5)).max() == 0 and np.abs(tile34(-5)).max() == 0
        m = np.concatenate(out, axis=0)
        c[f"w{tag}"] = halves(m) if f == 8 else three(m)
    spread = np.zeros((72, 32))
    spread[:64, :16] = np.kron(np.eye(8), np.eye(8)[:, :2])
    spread[64:66, 16:18] = np.eye(2)
    c["x34"] = np.concatenate([spread, spread], axis=1).astype(bf16)

    def pick(k, start, stop, rows_out, low_slots, high_slots):
        n = NROW >> k
        m = inverse_matrix(n)
        m[np.abs(m) < 1e-13] = 0.0
        base = mid * (BAND >> k)
        part = m[base + start : base + stop]
        low, high = part[:, : n // 2], part[:, n // 2 :]
        half = base // 2
        out = np.zeros((rows_out, len(low_slots)))
        seen = 0.0
        for i in range(len(low_slots)):
            if low_slots[i] is not None:
                out[: stop - start, i] += low[:, half + low_slots[i]]
            if high_slots[i] is not None:
                out[: stop - start, i] += high[:, half + high_slots[i]]
        want = (np.abs(low).sum() if any(s is not None for s in low_slots) else 0.0) + (
            np.abs(high).sum() if any(s is not None for s in high_slots) else 0.0
        )
        assert abs(want - np.abs(out).sum()) < 1e-9, k
        return out


    none = [None]
    bands = list(range(-3, 5))
    flat = lambda rows: sum(rows, [])
    l4 = flat([[b] + none * 7 for b in bands])
    h4 = flat([none + [b] + none * 6 for b in bands])
    c["s4"] = three(pick(4, -2, 6, 8, l4, h4))
    l3 = flat([none * 2 + [2 * b, 2 * b + 1] + none * 4 for b in bands])
    h3 = flat([none * 4 + [2 * b, 2 * b + 1] + none * 2 for b in bands])
    h3l = flat([none * 6 + [2 * b, 2 * b + 1] for b in bands])
    c["s3h"] = three(pick(3, -2, 8, 16, l3, h3))
    c["s3l"] = three(pick(3, -2, 8, 16, none * 64 + list(range(-2, 6)) + none * 8, h3l + none * 16))
    near = (-1, 0, 1)
    l2 = flat([[4 * b + i for i in range(4)] + none * 4 for b in near]) + none * 8
    h2 = flat([none * 4 + [4 * b + i for i in range(4)] for b in near]) + none * 8
    c["s2h"] = three(pick(2, -2, 12, 16, l2, h2))
    low_ext = [-2 + i if i < 10 else None for i in range(16)]
    ha = flat([[4 * b + i for i in range(4)] + none * 4 for b in near]) + none * 8
    hb = flat([none * 4 + [4 * b + i for i in range(4)] for b in near]) + none * 8
    c["s2l0"] = three(pick(2, -2, 12, 16, none * 32 + low_ext, ha + none * 16))
    c["s2l1"] = three(pick(2, -2, 12, 16, none * 32 + low_ext, hb + none * 16))
    s1 = list(range(8)) + list(range(-4, 0)) + list(range(8, 12))
    c["s1h"] = three(pick(1, -2, 18, 24, s1 + none * 16, none * 16 + s1))
    low_ext = [-2 + i if i < 14 else None for i in range(16)]
    c["s1l"] = three(pick(1, -2, 18, 24, low_ext + none * 16, none * 16 + s1))
    s0 = inner + edge + [-2, -1, 16, 17] + none * 4
    c["s0h"] = three(pick(0, 0, 32, 32, s0 + none * 24, none * 24 + s0))
    low_ext = [-2 + i if i < 20 else None for i in range(24)]
    c["s0l"] = three(pick(0, 0, 32, 32, low_ext + none * 24, none * 24 + s0))
    return c


GROUPS = (
    ("bf",),
    ("v0h", "v0l", "b4", "a1h", "a1l", "a2h", "a2l"),
    ("wm",),
    ("a0h", "a0l"),
    ("a0hi", "a0li", "a1hi", "a1li", "a2hi", "a2li", "wi"),
    ("u0h", "u0l", "u1h", "u1l", "u2h", "u2l", "x34", "u0hi", "u0li", "u1hi", "u1li", "u2hi", "u2li"),
    ("i4", "s4", "s3h", "s3l", "s2h", "s2l0", "s2l1", "s1h", "s1l", "s0h", "s0l"),
    ("bi",),
)


@functools.lru_cache(maxsize=None)
def packed():
    c = constants()
    assert sorted(sum(GROUPS, ())) == sorted(c)
    arrays, where = [], {}
    for g, names in enumerate(GROUPS):
        wide = max(-(-c[n].shape[1] // 128) * 128 for n in names)
        parts, at = [], 0
        for n in names:
            m = c[n]
            tall = -(-m.shape[0] // 16) * 16
            full = np.zeros((tall, wide), bf16)
            full[: m.shape[0], : m.shape[1]] = m
            parts.append(full)
            where[n] = (g, at, m.shape[0], m.shape[1])
            at += tall
        arrays.append(np.concatenate(parts, axis=0))
    return arrays, where


def split(x):
    hi = x.astype(bf16)
    return hi, (x - hi.astype(f32)).astype(bf16)


def dot(a, b):
    return jnp.dot(a, b, preferred_element_type=f32)


def rows(*parts):
    return jnp.concatenate(parts, axis=0)


def lanes(*parts):
    return jnp.concatenate(parts, axis=1) if len(parts) > 1 else parts[0]


COUNT = len(GROUPS)


def kernel(members_hbm, increment_hbm, weights_hbm, *refs):
    groups_hbm, out, groups = refs[:COUNT], refs[COUNT], refs[COUNT + 1 : 2 * COUNT + 1]
    (members, increment, weights, t_hi, t_lo, b_hi, b_lo, u_hi, u_lo,
     y0i, y0e, y1, yc, i0i, i0e, i1, ic,
     hs0, hs1, hs2, hr0, hr1, hr2, gs0, gs1, gs2, gr0, gr1, gr2,
     ks, kr, js, jr, qs, qr,
     e0i, e0e, e1, ce0i, ce0e, ce1, es0i, es0e, es1, es2, er0i, er0e, er1, er2,
     p0i, p0e, p1, pc, ss0, ss1, sr0, sr1, syc, srt,
     sem_s, sem_r, sem_l) = refs[2 * COUNT + 1 :]
    where = packed()[1]
    mem, tile = lax.axis_index("mem"), lax.axis_index("tile")
    ypos, core = lax.div(mem, 2), lax.rem(mem, 2)

    def at_tile(d):
        return (mem, lax.rem(tile + TILE + d, TILE))

    def at_y(j):
        return (lax.rem(ypos + j, 4) * 2 + core, tile)

    partner = (ypos * 2 + 1 - core, tile)
    near = [at_tile(d) for d in (1, -1, 2, -2, 3, -3, 4, -4)] + [partner] + [at_y(j) for j in (1, 2, 3)]
    barrier = pltpu.get_barrier_semaphore()
    for device in near:
        pl.semaphore_signal(barrier, inc=1, device_id=device, device_id_type=MESH)

    sources = [(groups_hbm[0], groups[0]), (members_hbm, members), (increment_hbm, increment)]
    sources += [(groups_hbm[g], groups[g]) for g in range(1, COUNT)] + [(weights_hbm, weights)]
    loads = [pltpu.make_async_copy(a, b, sem_l.at[n]) for n, (a, b) in enumerate(sources)]
    for load in loads:
        load.start()
    order = [0] + list(range(3, COUNT + 2))
    loaded = set()

    def need(n):
        if n not in loaded:
            loads[n].wait()
            loaded.add(n)

    def const(name):
        g, at, tall, wide = where[name]
        need(order[g])
        return groups[g][at : at + tall, :wide]

    def triple(name):
        m = const(name)
        half = m.shape[1] // 2
        return lanes(m[:, :half], m[:, :half], m[:, half:])

    sent = []

    def send(src, dst, device):
        n = len(sent)
        if n == 0:
            pl.semaphore_wait(barrier, len(near))
        copy = pltpu.make_async_remote_copy(
            src_ref=src, dst_ref=dst, send_sem=sem_s.at[n], recv_sem=sem_r.at[n], device_id=device, device_id_type=MESH
        )
        copy.start()
        sent.append(copy)
        return copy

    def window(ref, width, j, first, last):
        start = 256 * j - 128
        groups_ = []
        for t in [(start // 128 + i) % (width // 128) for i in range(4)]:
            if groups_ and groups_[-1][1] == t:
                groups_[-1][1] = t + 1
            else:
                groups_.append([t, t + 1])
        return lanes(*[ref[first:last, 128 * a : 128 * b] for a, b in groups_])

    def put(hi_ref, lo_ref, first, last, width, j, r):
        half = width // 2
        for ref, v in zip((hi_ref, lo_ref), split(r)):
            ref[first:last, 128 * j : 128 * j + 128] = v[:, :128]
            ref[first:last, half + 128 * j : half + 128 * j + 128] = v[:, 128:]

    base = [0, 2048, 3072, 3584, 3840]
    bf = const("bf")
    bf_hi, bf_lo = bf[:512], bf[512:]
    need(1)
    for j in range(8):
        w = window(members, 2048, j, 0, 256)
        r = dot(w, bf_hi) + dot(w, bf_lo)
        put(t_hi, t_lo, 0, 256, 2048, j, r)
        r = r.reshape(8, 32, 256)
        put(b_hi, b_lo, 0, 128, 2048, j, rows(r[:, 24:].reshape(64, 256), r[:, :8].reshape(64, 256)))

    def part(k, which, first, last):
        half = 1024 >> k
        s = base[k] + (half if which == "h" else 0)
        hi, lo = t_hi[first:last, s : s + half], t_lo[first:last, s : s + half]
        return rows(hi, lo, hi)

    owed = {}
    for which, s in (("h", 1024), ("l", 0)):
        hi, lo = b_hi[:, s : s + 1024], b_lo[:, s : s + 1024]
        owed[which] = dot(triple("v0" + which), rows(hi, lo, hi))
    halos = [[], [], []]

    def share(k, h, l, hs, hr):
        half = h.shape[0] // 2
        for n, d in enumerate((1, -1)):
            hs[n] = rows(h[n * half : n * half + half], l[n * half : n * half + half]).astype(bf16)
            halos[k].append(send(hs.at[n], hr.at[n], at_tile(d)))

    share(0, owed["h"], owed["l"], hs0, hr0)

    need(2)
    hi, lo = split(increment[...])
    u_hi[...], u_lo[...] = hi, lo
    a = rows(*[window(u_hi, 2048, j, 0, 32) for j in range(8)])
    b = rows(*[window(u_lo, 2048, j, 0, 32) for j in range(8)])
    r = dot(rows(a, b), bf_hi)
    r = r[:256] + r[256:] + dot(a, bf_lo)
    for j in range(8):
        put(t_hi, t_lo, 256, 288, 2048, j, r[32 * j : 32 * j + 32])

    def down(k):
        width, s = 2048 >> k, base[k - 1]
        if k < 4:
            for j in range(width // 256):
                a = window(t_hi.at[:, s : s + width], width, j, 0, 288)
                b = window(t_lo.at[:, s : s + width], width, j, 0, 288)
                r = dot(a, bf_hi) + dot(b, bf_hi) + dot(a, bf_lo)
                put(t_hi.at[:, base[k] : base[k] + width], t_lo.at[:, base[k] : base[k] + width], 0, 288, width, j, r)
        else:
            m = const("b4")
            a, b = t_hi[:, s : s + 128], t_lo[:, s : s + 128]
            hi, lo = split(dot(a, m[:128]) + dot(b, m[:128]) + dot(a, m[128:]))
            t_hi[:, base[4] : base[4] + 128] = hi
            t_lo[:, base[4] : base[4] + 128] = lo

    down(1)
    h = dot(triple("a1h"), part(1, "h", 0, 256))
    l = dot(triple("a1l"), part(1, "l", 0, 256))
    share(1, h[128:], l[64:], hs1, hr1)
    y1[:, 0:512], y1[:, 512:1024], y1[:, 1024:] = h[:64], h[64:128], l[:64]
    down(2)
    h = dot(triple("a2h"), part(2, "h", 0, 256))
    l = dot(triple("a2l"), part(2, "l", 0, 256))
    share(2, h[64:], l[128:], hs2, hr2)
    yc[:, 0:256], yc[:, 256:384] = h[:64], l[:64, :128] + l[64:128, 128:]
    down(3)
    down(4)

    def stack34(first, last):
        hi = rows(*[t_hi[first:last, s : s + 128] for s in (base[4], base[3] + 128, base[3])])
        lo = rows(*[t_lo[first:last, s : s + 128] for s in (base[4], base[3] + 128, base[3])])
        return rows(hi, lo, hi)

    wm = dot(triple("wm"), stack34(0, 256))
    wi = dot(const("wi"), stack34(256, 288))
    yc[:, 384:] = wm[0:64]
    ic[:, 384:] = wi[0:8]
    far = []
    for n, d in enumerate((1, -1)):
        ks[n] = rows(wm[64 + 64 * n : 128 + 64 * n], wi[8 + 8 * n : 16 + 8 * n])
        far.append(send(ks.at[n], kr.at[n], at_tile(d)))
    z8 = jnp.zeros((8, 128), f32)
    for n, d in enumerate((2, -2)):
        js[n] = rows(wm[192 + 64 * n : 256 + 64 * n], wi[24 + 8 * n : 32 + 8 * n], z8).astype(bf16)
        far.append(send(js.at[n], jr.at[n], at_tile(d)))
    for n, d in enumerate((3, -3, 4)):
        qs[n] = rows(wm[320 + 16 * n : 336 + 16 * n], wi[40 + 8 * n : 48 + 8 * n], z8).astype(bf16)
        far.append(send(qs.at[n], qr.at[n], at_tile(d)))

    y = dot(triple("a0h"), part(0, "h", 0, 256))
    x = dot(triple("a0l"), part(0, "l", 0, 256))
    for n, v in enumerate((y[:64], y[64:128], x[:64])):
        e0i[:, :, :, 1024 * n : 1024 * n + 1024] = (v * v).reshape(4, 2, 8, 1024)
    pair0i = send(e0i.at[:, 1 - core], ce0i, partner)
    y0e[:, 0:1024], y0e[:, 1024:2048], y0e[:, 2048:] = y[128:192], y[192:], x[64:]

    gifts = [[], [], []]

    def give(k, n8, p8, gs, gr):
        tall = gs.shape[1]
        for n, (d, v) in enumerate(((1, n8), (-1, p8))):
            gs[n] = v[:tall]
            gifts[k].append(send(gs.at[n], gr.at[n], at_tile(d)))

    y = dot(const("a0hi"), part(0, "h", 256, 288))
    x = dot(const("a0li"), part(0, "l", 256, 288))
    give(0, y[32:40] + x[16:24], y[40:48] + x[24:32], gs0, gr0)
    i0i[:, 0:1024], i0i[:, 1024:2048], i0i[:, 2048:] = y[:8], y[8:16], x[:8]
    i0e[:, 0:1024], i0e[:, 1024:2048], i0e[:, 2048:] = y[16:24], y[24:32], x[8:16]
    y = dot(const("a1hi"), part(1, "h", 256, 288))
    x = dot(const("a1li"), part(1, "l", 256, 288))
    give(1, y[16:24] + x[8:16], y[24:32] + x[16:24], gs1, gr1)
    i1[:, 0:512], i1[:, 512:1024], i1[:, 1024:] = y[:8], y[8:16], x[:8]
    y = dot(const("a2hi"), part(2, "h", 256, 288))
    x = dot(const("a2li"), part(2, "l", 256, 288))
    give(2, y[8:16] + x[16:24], y[16:24] + x[24:32], gs2, gr2)
    ic[:, 0:256], ic[:, 256:384] = y[:8], x[:8, :128] + x[8:16, 128:]

    def fold(v):
        half = v.shape[1] // 2
        v = v * v
        return rows(v[:, :half], v[:, half:]).astype(bf16)

    def unfold(v):
        v = jnp.sqrt(v.astype(f32))
        return lanes(v[:8], v[8:])

    def along_y(e, ce, es, er):
        copies = []
        for j in (2, 1, 3):
            q = lax.rem(ypos + j, 4)
            es[j - 1] = fold(e[q, core] + ce[q])
            copies.append(send(es.at[j - 1], er.at[j - 1], at_y(j)))
        return copies

    def total(e, ce, er, copies):
        v = e[ypos, core] + ce[ypos]
        for copy in copies:
            copy.wait_recv()
        return v + unfold(er[0]) + unfold(er[1]) + unfold(er[2])

    pair0i.wait_recv()
    over0i = along_y(e0i, ce0i, es0i, er0i)

    def got(k, ref):
        for copy in halos[k]:
            copy.wait_recv()
        a, b = ref[0], ref[1]
        return rows(a, b, a, b)

    g = got(0, hr0)
    q = dot(const("u0h"), g)
    x = dot(const("u0l"), g)
    for n, v in enumerate((q[:64], q[64:], x)):
        v = v + y0e[:, 1024 * n : 1024 * n + 1024]
        e0e[:, :, :, 1024 * n : 1024 * n + 1024] = (v * v).reshape(4, 2, 8, 1024)
    pair0e = send(e0e.at[:, 1 - core], ce0e, partner)

    g = got(1, hr1)
    q = dot(const("u1h"), g)
    x = dot(const("u1l"), g)
    for n, v in enumerate((q[:64], q[64:], x)):
        v = v + y1[:, 512 * n : 512 * n + 512]
        e1[:, :, :, 512 * n : 512 * n + 512] = (v * v).reshape(4, 2, 8, 512)
    g = got(2, hr2)
    v = yc[:, 0:256] + dot(const("u2h"), g)
    e1[:, :, :, 1536:1792] = (v * v).reshape(4, 2, 8, 256)
    x = dot(const("u2l"), g)
    v = yc[:, 256:384] + x[:64, :128] + x[64:, 128:]
    e1[:, :, :, 1792:1920] = (v * v).reshape(4, 2, 8, 128)
    for copy in far:
        copy.wait_recv()
    q = qr[0].astype(f32) + qr[1].astype(f32) + qr[2].astype(f32)
    v34 = kr[0] + kr[1] + (jr[0].astype(f32) + jr[1].astype(f32))[:72] + dot(const("x34"), rows(*split(q)))
    v = yc[:, 384:] + v34[:64]
    e1[:, :, :, 1920:] = (v * v).reshape(4, 2, 8, 128)
    pair1 = send(e1.at[:, 1 - core], ce1, partner)

    pair0e.wait_recv()
    over0e = along_y(e0e, ce0e, es0e, er0e)

    def taken(k, ref):
        for copy in gifts[k]:
            copy.wait_recv()
        a, b = ref[0], ref[1]
        z = [jnp.zeros((8, a.shape[1]), f32)] * (a.shape[0] == 4)
        hi, lo = split(rows(a, b, *z))
        return rows(hi, lo, hi)

    g = taken(0, gr0)
    q = dot(const("u0hi"), g)
    i0e[:, 0:1024] += q[:8]
    i0e[:, 1024:2048] += q[8:]
    i0e[:, 2048:] += dot(const("u0li"), g)
    g = taken(1, gr1)
    q = dot(const("u1hi"), g)
    i1[:, 0:512] += q[:8]
    i1[:, 512:1024] += q[8:]
    i1[:, 1024:] += dot(const("u1li"), g)
    g = taken(2, gr2)
    ic[:, 0:256] += dot(const("u2hi"), g)
    x = dot(const("u2li"), g)
    ic[:, 256:384] += x[:8, :128] + x[8:, 128:]
    ic[:, 384:] += v34[64:72]

    pair1.wait_recv()
    over1 = []
    for j in (2, 1, 3):
        q = lax.rem(ypos + j, 4)
        both = e1[q, core] + ce1[q]
        es2[j - 1] = both[:, 1536:]
        over1.append(send(es2.at[j - 1], er2.at[j - 1], at_y(j)))
        es1[j - 1] = fold(both[:, :1536])
        over1.append(send(es1.at[j - 1], er1.at[j - 1], at_y(j)))

    need(COUNT + 2)
    w = [weights[i] * (1.0 / (MEM - 1)) for i in range(16)]

    def scaled(energy, ref, k):
        third = ref.shape[1] // 3
        return [w[3 * k + j] * energy[:, third * n : third * n + third] * ref[:, third * n : third * n + third] for n, j in enumerate((0, 2, 1))]

    def keep(ref, values):
        third = ref.shape[1] // 3
        for n, v in enumerate(values):
            ref[:, third * n : third * n + third] = v

    keep(p0i, scaled(total(e0i, ce0i, er0i, over0i), i0i, 0))
    keep(p0e, scaled(total(e0e, ce0e, er0e, over0e), i0e, 0))
    ss0[0] = p0e[6:8]
    ss0[1] = p0e[0:2]
    syn0 = [send(ss0.at[n], sr0.at[n], at_tile(d)) for n, d in enumerate((1, -1))]

    v = e1[ypos, core] + ce1[ypos]
    for copy in over1:
        copy.wait_recv()
    energy = v[:, 1536:] + er2[0] + er2[1] + er2[2]
    row = lax.broadcasted_iota(jnp.int32, (8, 128), 0)
    lane = lax.broadcasted_iota(jnp.int32, (8, 128), 1)
    w34 = jnp.where(
        row < 2,
        jnp.where(row == 0, jnp.where(lane < 64, w[15], w[12]), jnp.where(lane < 64, w[13], w[14])),
        jnp.where(row < 4, w[9], jnp.where(row < 6, w[11], w[10])),
    )
    w2 = jnp.where(lax.broadcasted_iota(jnp.int32, (8, 256), 0) < 4, w[6], w[8])
    pc[:, 0:256] = w2 * energy[:, 0:256] * ic[:, 0:256]
    pc[:, 256:384] = w[7] * energy[:, 256:384] * ic[:, 256:384]
    pc[:, 384:] = w34 * energy[:, 384:] * ic[:, 384:]
    synt = [send(pc.at[:, 384:], srt.at[n], at_tile(d)) for n, d in enumerate((2, -2, 3, -3, -4))]
    sync = [send(pc, syc.at[n], at_tile(d)) for n, d in enumerate((1, -1))]
    energy = v[:, :1536] + unfold(er1[0]) + unfold(er1[1]) + unfold(er1[2])
    keep(p1, scaled(energy, i1, 1))
    ss1[0] = p1[4:8]
    ss1[1] = p1[0:4]
    syn1 = [send(ss1.at[n], sr1.at[n], at_tile(d)) for n, d in enumerate((1, -1))]

    bi = const("bi")
    bi_hi, bi_lo = bi[:768], bi[768:]

    def left(name, x):
        hi, lo = split(x)
        return dot(const(name), rows(hi, lo, hi))

    def columns(x):
        tall, half = x.shape[0], x.shape[1] // 2
        count = half // 128

        def win(j):
            return lanes(*[x[:, s + 128 * ((j + i) % count) : s + 128 * ((j + i) % count) + 128] for s in (0, half) for i in (-1, 0, 1)])

        a, b = split(rows(*[win(j) for j in range(count)]))
        r = dot(rows(a, b), bi_hi)
        r = r[: tall * count] + r[tall * count :] + dot(a, bi_lo)
        return lanes(*[r[tall * j : tall * j + tall] for j in range(count)])

    for copy in synt + sync:
        copy.wait_recv()
    t = {-2: srt[0], 2: srt[1], -3: srt[2], 3: srt[3], 4: srt[4], 0: pc[:, 384:], -1: syc[0, :, 384:], 1: syc[1, :, 384:]}
    stack = rows(*[t[b] for b in range(-3, 5)])
    hi, lo = split(left("s4", stack))
    m = const("i4")
    ll3 = dot(hi, m[:128]) + dot(lo, m[:128]) + dot(hi, m[128:])
    ll2 = columns(lanes(left("s3l", rows(stack, ll3, z8)), left("s3h", stack)))
    stack = rows(syc[0, :, 0:384], pc[:, 0:384], syc[1, :, 0:384], jnp.zeros((8, 384), f32))
    ll1 = columns(lanes(
        left("s2l0", rows(stack[:, 256:384], ll2[:, :128])),
        left("s2l1", rows(stack[:, 256:384], ll2[:, 128:])),
        left("s2h", stack[:, :256]),
    ))
    for copy in syn1:
        copy.wait_recv()
    stack = rows(p1[...], sr1[0], sr1[1])
    ll0 = columns(lanes(
        left("s1l", rows(ll1, stack[:, 1024:])),
        left("s1h", rows(stack[:, 0:512], stack[:, 512:1024])),
    ))
    for copy in syn0:
        copy.wait_recv()
    stack = rows(p0i[...], p0e[...], sr0[0], sr0[1], jnp.zeros((4, 3072), f32))
    out[...] = columns(lanes(
        left("s0l", rows(ll0, stack[:, 2048:])),
        left("s0h", rows(stack[:, 0:1024], stack[:, 1024:2048])),
    ))
    for copy in sent:
        copy.wait_send()


def local(members, increment, weights):
    arrays = packed()[0]
    anywhere = pl.BlockSpec(memory_space=pl.ANY)
    v = pltpu.VMEM
    scratch = [v(a.shape, bf16) for a in arrays] + [
        v((256, 2048), bf16), v((BAND, 2048), f32), pltpu.SMEM((16,), f32),
        v((288, 3968), bf16), v((288, 3968), bf16), v((128, 2048), bf16), v((128, 2048), bf16), v((32, 2048), bf16), v((32, 2048), bf16),
        v((8, 128), f32), v((64, 3072), f32), v((64, 1536), f32), v((64, 512), f32),
        v((8, 3072), f32), v((8, 3072), f32), v((8, 1536), f32), v((8, 512), f32),
        v((2, 32, 1024), bf16), v((2, 48, 512), bf16), v((2, 64, 256), bf16),
        v((2, 32, 1024), bf16), v((2, 48, 512), bf16), v((2, 64, 256), bf16),
        v((2, 4, 1024), f32), v((2, 8, 512), f32), v((2, 8, 256), f32),
        v((2, 4, 1024), f32), v((2, 8, 512), f32), v((2, 8, 256), f32),
        v((2, 72, 128), f32), v((2, 72, 128), f32), v((2, 80, 128), bf16), v((2, 80, 128), bf16), v((3, 32, 128), bf16), v((3, 32, 128), bf16),
        v((4, 2, 8, 3072), f32), v((4, 2, 8, 3072), f32), v((4, 2, 8, 2048), f32),
        v((4, 8, 3072), f32), v((4, 8, 3072), f32), v((4, 8, 2048), f32),
        v((3, 16, 1536), bf16), v((3, 16, 1536), bf16), v((3, 16, 768), bf16), v((3, 8, 512), f32),
        v((3, 16, 1536), bf16), v((3, 16, 1536), bf16), v((3, 16, 768), bf16), v((3, 8, 512), f32),
        v((8, 3072), f32), v((8, 3072), f32), v((8, 1536), f32), v((8, 512), f32),
        v((2, 2, 3072), f32), v((2, 4, 1536), f32), v((2, 2, 3072), f32), v((2, 4, 1536), f32),
        v((2, 8, 512), f32), v((5, 8, 128), f32),
        pltpu.SemaphoreType.DMA((48,)), pltpu.SemaphoreType.DMA((48,)), pltpu.SemaphoreType.DMA((COUNT + 3,)),
    ]
    result = pl.pallas_call(
        kernel,
        out_shape=jax.ShapeDtypeStruct((BAND, 2048), f32),
        in_specs=[anywhere] * (3 + COUNT),
        out_specs=pl.BlockSpec(memory_space=pltpu.VMEM),
        scratch_shapes=scratch,
        compiler_params=pltpu.CompilerParams(collective_id=0, has_side_effects=True, vmem_limit_bytes=56 * 2**20),
    )(members.reshape(256, 2048), increment.reshape(BAND, 2048), weights, *[jnp.asarray(a) for a in arrays])
    return result.reshape(1, BAND, 2048)


def solution(mesh):
    return jax.shard_map(
        local,
        mesh=mesh,
        in_specs=(P("mem", None, "tile", None), P("mem", "tile", None), P()),
        out_specs=P("mem", "tile", None),
        check_vma=False,
    )
```

time: 43.3 us -> 36.6 us (0.85); the launches traced: 42.7 us -> 36.5 us
  Pallas kernels: 41 us -> 34.8 us
    pallas_call x1, Pallas kernels: 41 us -> 34.8 us  [local(): pl.pallas_call(kernel, out_shape=jax.ShapeDtypeStruct((BAND, 2048), f32),...]
where the time goes in v2:
time: 36.6 us; the launch traced here: 36.5 us
  Pallas kernels  34.8 us (95%)
  local copies, waits for them, and re-layouts  1.67 us (5%)
    pallas_call x1, Pallas kernels, local(): pl.pallas_call(kernel, out_shape=jax.ShapeDtypeStruct((BAND, 2048), f32),...  34.8 us
    unnamed x1, local copies, waits for them, and re-layouts  1.67 us

profile of v2, /device:TPU:1, one launch (start us, length us, event | category | flops | bytes accessed | tf_op | source)
XLA Modules:
  0.0 36.5 jit_solution(14641452671072910055)
XLA Ops:
  0.0 34.8 %shard_map.109 = f32[32,2048]{1,0:T(8,128)} custom-call(bf16[256,2048]{1,0:T(8,128)(2,1)} %bitcast.4, f32[32,2048]{1,0:T(8,128)} %bitcast.5, f32[16]{0:T(128)} %weights_hbm.1, bf16[1024,256]{1,0:T(8,128)(2,1)} %constant.16.clone.refs_0_, bf16[928,512]{1,0:T(8,128)(2,1)} %constant.17.clone.refs_1_, bf16[368,1536]{1,0:T(8,128)(2,1)} %constant.18.clone.refs_2_, ...), custom_call_target="tpu_custom_call" | custom-call | tf_op jit(solution)/shard_map/pallas_call | solution.py:712
  34.8 1.7 %copy.13 = f32[1,32,2048]{2,1,0:T(8,128)} copy(f32[1,32,2048]{2,1,0:T(8,128)} %bitcast.3) | data formatting | bytes 524288

commit v3 on v2

--- a/solution.py
+++ b/solution.py
@@ -89,12 +89,14 @@
     lo2048, hi2048 = forward_matrix(2048)
     bf = np.concatenate([lo2048[512:640, 896:1408], hi2048[512:640, 896:1408]], axis=0).T
     c["bf"] = np.concatenate(pieces(bf), axis=0)
+    l256, h256 = forward_matrix(256)
     l128, h128 = forward_matrix(128)
-    c["b4"] = np.concatenate(pieces(np.concatenate([l128, h128], axis=0).T), axis=0)
+    c["b34"] = np.concatenate(pieces(np.concatenate([l128 @ l256, h128 @ l256, h256, l256], axis=0).T), axis=0)
     s2048 = inverse_matrix(2048)
     bi = np.concatenate([s2048[1024:1280, 384:768], s2048[1024:1280, 1024 + 384 : 1024 + 768]], axis=1).T
     c["bi"] = np.concatenate(pieces(bi), axis=0)
-    c["i4"] = np.concatenate(pieces(inverse_matrix(128).T), axis=0)
+    s256 = inverse_matrix(256).T
+    c["i34"] = np.concatenate(pieces(np.concatenate([inverse_matrix(128).T @ s256[:128], s256], axis=0)), axis=0)
 
     inner, edge = list(range(4, 12)), [0, 1, 2, 3, 12, 13, 14, 15]
     for k in range(3):
@@ -191,9 +193,7 @@
         assert np.abs(tile34(-4)).max() == 0 and np.abs(tile34(5)).max() == 0 and np.abs(tile34(-5)).max() == 0
         m = np.concatenate(out, axis=0)
         c[f"w{tag}"] = halves(m) if f == 8 else three(m)
-    spread = np.zeros((72, 32))
-    spread[:64, :16] = np.kron(np.eye(8), np.eye(8)[:, :2])
-    spread[64:66, 16:18] = np.eye(2)
+    spread = np.kron(np.eye(8), np.eye(8)[:, :2])
     c["x34"] = np.concatenate([spread, spread], axis=1).astype(bf16)
 
     def pick(k, start, stop, rows_out, low_slots, high_slots):
@@ -223,12 +223,12 @@
     flat = lambda rows: sum(rows, [])
     l4 = flat([[b] + none * 7 for b in bands])
     h4 = flat([none + [b] + none * 6 for b in bands])
-    c["s4"] = three(pick(4, -2, 6, 8, l4, h4))
+    m4 = pick(4, -2, 6, 8, l4, h4)
     l3 = flat([none * 2 + [2 * b, 2 * b + 1] + none * 4 for b in bands])
     h3 = flat([none * 4 + [2 * b, 2 * b + 1] + none * 2 for b in bands])
     h3l = flat([none * 6 + [2 * b, 2 * b + 1] for b in bands])
-    c["s3h"] = three(pick(3, -2, 8, 16, l3, h3))
-    c["s3l"] = three(pick(3, -2, 8, 16, none * 64 + list(range(-2, 6)) + none * 8, h3l + none * 16))
+    low3 = pick(3, -2, 8, 16, list(range(-2, 6)), none * 8)
+    c["s34"] = three(np.concatenate([low3 @ m4, pick(3, -2, 8, 16, none * 64, h3l), pick(3, -2, 8, 16, l3, h3)], axis=0))
     near = (-1, 0, 1)
     l2 = flat([[4 * b + i for i in range(4)] + none * 4 for b in near]) + none * 8
     h2 = flat([none * 4 + [4 * b + i for i in range(4)] for b in near]) + none * 8
@@ -236,27 +236,29 @@
     low_ext = [-2 + i if i < 10 else None for i in range(16)]
     ha = flat([[4 * b + i for i in range(4)] + none * 4 for b in near]) + none * 8
     hb = flat([none * 4 + [4 * b + i for i in range(4)] for b in near]) + none * 8
-    c["s2l0"] = three(pick(2, -2, 12, 16, none * 32 + low_ext, ha + none * 16))
-    c["s2l1"] = three(pick(2, -2, 12, 16, none * 32 + low_ext, hb + none * 16))
+    c["s2x"] = three(pick(2, -2, 12, 16, low_ext, none * 16))
+    c["s2p"] = three(np.concatenate([pick(2, -2, 12, 16, none * 32, ha), pick(2, -2, 12, 16, none * 32, hb)], axis=0))
     s1 = list(range(8)) + list(range(-4, 0)) + list(range(8, 12))
     c["s1h"] = three(pick(1, -2, 18, 24, s1 + none * 16, none * 16 + s1))
     low_ext = [-2 + i if i < 14 else None for i in range(16)]
-    c["s1l"] = three(pick(1, -2, 18, 24, low_ext + none * 16, none * 16 + s1))
-    s0 = inner + edge + [-2, -1, 16, 17] + none * 4
-    c["s0h"] = three(pick(0, 0, 32, 32, s0 + none * 24, none * 24 + s0))
-    low_ext = [-2 + i if i < 20 else None for i in range(24)]
-    c["s0l"] = three(pick(0, 0, 32, 32, low_ext + none * 24, none * 24 + s0))
+    c["s1x"] = three(pick(1, -2, 18, 24, low_ext, none * 16))
+    c["s1p"] = three(pick(1, -2, 18, 24, none * 16, s1))
+    s0 = inner + edge + [-2, -1, 16, 17] + none * 12
+    c["s0h"] = three(pick(0, 0, 32, 32, s0 + none * 32, none * 32 + s0))
+    low_ext = [-2 + i if i < 20 else None for i in range(32)]
+    c["s0x"] = three(pick(0, 0, 32, 32, low_ext, none * 32))
+    c["s0p"] = three(pick(0, 0, 32, 32, none * 32, s0))
     return c
 
 
 GROUPS = (
     ("bf",),
-    ("v0h", "v0l", "b4", "a1h", "a1l", "a2h", "a2l"),
+    ("v0h", "v0l", "b34", "a1h", "a1l", "a2h", "a2l"),
     ("wm",),
     ("a0h", "a0l"),
     ("a0hi", "a0li", "a1hi", "a1li", "a2hi", "a2li", "wi"),
     ("u0h", "u0l", "u1h", "u1l", "u2h", "u2l", "x34", "u0hi", "u0li", "u1hi", "u1li", "u2hi", "u2li"),
-    ("i4", "s4", "s3h", "s3l", "s2h", "s2l0", "s2l1", "s1h", "s1l", "s0h", "s0l"),
+    ("i34", "s34", "s2h", "s2x", "s2p", "s1h", "s1x", "s1p", "s0h", "s0x", "s0p"),
     ("bi",),
 )
 
@@ -299,16 +301,17 @@
 
 
 COUNT = len(GROUPS)
+NEXT, FAR = (1, -1), (2, -2, 3, -3, -4)
 
 
 def kernel(members_hbm, increment_hbm, weights_hbm, *refs):
     groups_hbm, out, groups = refs[:COUNT], refs[COUNT], refs[COUNT + 1 : 2 * COUNT + 1]
     (members, increment, weights, t_hi, t_lo, b_hi, b_lo, u_hi, u_lo,
-     y0i, y0e, y1, yc, i0i, i0e, i1, ic,
+     y0e, y1, yc, i0i, i0e, i1, ic,
      hs0, hs1, hs2, hr0, hr1, hr2, gs0, gs1, gs2, gr0, gr1, gr2,
-     ks, kr, js, jr, qs, qr,
-     e0i, e0e, e1, ce0i, ce0e, ce1, es0i, es0e, es1, es2, er0i, er0e, er1, er2,
-     p0i, p0e, p1, pc, ss0, ss1, sr0, sr1, syc, srt,
+     ks, kr, js, jr, qs, qr, gks, gkr,
+     e0i, e0e, e1, ec, ce0i, ce0e, ce1, cec, es0i, es0e, es1, es2, er0i, er0e, er1, er2,
+     syc, srt, p0i, p0e, p1, pc, ss0, ss1, sr0, sr1,
      sem_s, sem_r, sem_l) = refs[2 * COUNT + 1 :]
     where = packed()[1]
     mem, tile = lax.axis_index("mem"), lax.axis_index("tile")
@@ -329,10 +332,13 @@
     sources = [(groups_hbm[0], groups[0]), (members_hbm, members), (increment_hbm, increment)]
     sources += [(groups_hbm[g], groups[g]) for g in range(1, COUNT)] + [(weights_hbm, weights)]
     loads = [pltpu.make_async_copy(a, b, sem_l.at[n]) for n, (a, b) in enumerate(sources)]
-    for load in loads:
-        load.start()
     order = [0] + list(range(3, COUNT + 2))
-    loaded = set()
+    begun, loaded = set(), set()
+
+    def begin(*which):
+        for n in which:
+            loads[n].start()
+            begun.add(n)
 
     def need(n):
         if n not in loaded:
@@ -378,10 +384,12 @@
             ref[first:last, 128 * j : 128 * j + 128] = v[:, :128]
             ref[first:last, half + 128 * j : half + 128 * j + 128] = v[:, 128:]
 
-    base = [0, 2048, 3072, 3584, 3840]
+    base = [0, 2048, 3072]
+    begin(0, 1)
     bf = const("bf")
     bf_hi, bf_lo = bf[:512], bf[512:]
     need(1)
+    begin(3, 4, 2, 5, 6, 7)
     for j in range(8):
         w = window(members, 2048, j, 0, 256)
         r = dot(w, bf_hi) + dot(w, bf_lo)
@@ -408,6 +416,57 @@
             halos[k].append(send(hs.at[n], hr.at[n], at_tile(d)))
 
     share(0, owed["h"], owed["l"], hs0, hr0)
+
+    def down(k, first, last):
+        width, s = 2048 >> k, base[k - 1]
+        tall, count = last - first, width // 256
+        each = 1 if tall > 32 else count
+        for j in range(0, count, each):
+            a = rows(*[window(t_hi.at[:, s : s + width], width, i, first, last) for i in range(j, j + each)])
+            b = rows(*[window(t_lo.at[:, s : s + width], width, i, first, last) for i in range(j, j + each)])
+            r = dot(a, bf_hi) + dot(b, bf_hi) + dot(a, bf_lo)
+            for i in range(each):
+                put(t_hi.at[:, base[k] : base[k] + width], t_lo.at[:, base[k] : base[k] + width], first, last, width, j + i, r[tall * i : tall * i + tall])
+
+    begin(*range(8, COUNT + 3))
+    down(1, 0, 256)
+    share(1, dot(triple("a1h")[128:], part(1, "h", 0, 256)), dot(triple("a1l")[64:], part(1, "l", 0, 256)), hs1, hr1)
+    down(2, 0, 256)
+    share(2, dot(triple("a2h")[64:], part(2, "h", 0, 256)), dot(triple("a2l")[128:], part(2, "l", 0, 256)), hs2, hr2)
+
+    def stack34(first, last):
+        m, s = const("b34"), base[2]
+        a, b = t_hi[first:last, s : s + 256], t_lo[first:last, s : s + 256]
+        r = dot(a, m[:256]) + dot(b, m[:256]) + dot(a, m[256:])
+        hi, lo = split(rows(r[:, :128], r[:, 128:256], r[:, 256:]))
+        return rows(hi, lo, hi)
+
+    wm = dot(triple("wm"), stack34(0, 256))
+    yc[:, 384:] = wm[0:64]
+    far = []
+    for n, d in enumerate((1, -1)):
+        ks[n] = wm[64 + 64 * n : 128 + 64 * n]
+        far.append(send(ks.at[n], kr.at[n], at_tile(d)))
+    for n, d in enumerate((2, -2)):
+        js[n] = wm[192 + 64 * n : 256 + 64 * n].astype(bf16)
+        far.append(send(js.at[n], jr.at[n], at_tile(d)))
+    for n, d in enumerate((3, -3, 4)):
+        qs[n] = wm[320 + 16 * n : 336 + 16 * n].astype(bf16)
+        far.append(send(qs.at[n], qr.at[n], at_tile(d)))
+
+    y = dot(triple("a0h"), part(0, "h", 0, 256))
+    x = dot(triple("a0l"), part(0, "l", 0, 256))
+    for n, v in enumerate((y[:64], y[64:128], x[:64])):
+        e0i[:, :, :, 1024 * n : 1024 * n + 1024] = (v * v).reshape(4, 2, 8, 1024)
+    pair0i = send(e0i.at[:, 1 - core], ce0i, partner)
+    y0e[:, 0:1024], y0e[:, 1024:2048], y0e[:, 2048:] = y[128:192], y[192:], x[64:]
+
+    h = dot(triple("a1h")[:128], part(1, "h", 0, 256))
+    l = dot(triple("a1l")[:64], part(1, "l", 0, 256))
+    y1[:, 0:512], y1[:, 512:1024], y1[:, 1024:] = h[:64], h[64:], l
+    h = dot(triple("a2h")[:64], part(2, "h", 0, 256))
+    l = dot(triple("a2l")[:128], part(2, "l", 0, 256))
+    yc[:, 0:256], yc[:, 256:384] = h, l[:64, :128] + l[64:, 128:]
 
     need(2)
     hi, lo = split(increment[...])
@@ -418,63 +477,8 @@
     r = r[:256] + r[256:] + dot(a, bf_lo)
     for j in range(8):
         put(t_hi, t_lo, 256, 288, 2048, j, r[32 * j : 32 * j + 32])
-
-    def down(k):
-        width, s = 2048 >> k, base[k - 1]
-        if k < 4:
-            for j in range(width // 256):
-                a = window(t_hi.at[:, s : s + width], width, j, 0, 288)
-                b = window(t_lo.at[:, s : s + width], width, j, 0, 288)
-                r = dot(a, bf_hi) + dot(b, bf_hi) + dot(a, bf_lo)
-                put(t_hi.at[:, base[k] : base[k] + width], t_lo.at[:, base[k] : base[k] + width], 0, 288, width, j, r)
-        else:
-            m = const("b4")
-            a, b = t_hi[:, s : s + 128], t_lo[:, s : s + 128]
-            hi, lo = split(dot(a, m[:128]) + dot(b, m[:128]) + dot(a, m[128:]))
-            t_hi[:, base[4] : base[4] + 128] = hi
-            t_lo[:, base[4] : base[4] + 128] = lo
-
-    down(1)
-    h = dot(triple("a1h"), part(1, "h", 0, 256))
-    l = dot(triple("a1l"), part(1, "l", 0, 256))
-    share(1, h[128:], l[64:], hs1, hr1)
-    y1[:, 0:512], y1[:, 512:1024], y1[:, 1024:] = h[:64], h[64:128], l[:64]
-    down(2)
-    h = dot(triple("a2h"), part(2, "h", 0, 256))
-    l = dot(triple("a2l"), part(2, "l", 0, 256))
-    share(2, h[64:], l[128:], hs2, hr2)
-    yc[:, 0:256], yc[:, 256:384] = h[:64], l[:64, :128] + l[64:128, 128:]
-    down(3)
-    down(4)
-
-    def stack34(first, last):
-        hi = rows(*[t_hi[first:last, s : s + 128] for s in (base[4], base[3] + 128, base[3])])
-        lo = rows(*[t_lo[first:last, s : s + 128] for s in (base[4], base[3] + 128, base[3])])
-        return rows(hi, lo, hi)
-
-    wm = dot(triple("wm"), stack34(0, 256))
-    wi = dot(const("wi"), stack34(256, 288))
-    yc[:, 384:] = wm[0:64]
-    ic[:, 384:] = wi[0:8]
-    far = []
-    for n, d in enumerate((1, -1)):
-        ks[n] = rows(wm[64 + 64 * n : 128 + 64 * n], wi[8 + 8 * n : 16 + 8 * n])
-        far.append(send(ks.at[n], kr.at[n], at_tile(d)))
-    z8 = jnp.zeros((8, 128), f32)
-    for n, d in enumerate((2, -2)):
-        js[n] = rows(wm[192 + 64 * n : 256 + 64 * n], wi[24 + 8 * n : 32 + 8 * n], z8).astype(bf16)
-        far.append(send(js.at[n], jr.at[n], at_tile(d)))
-    for n, d in enumerate((3, -3, 4)):
-        qs[n] = rows(wm[320 + 16 * n : 336 + 16 * n], wi[40 + 8 * n : 48 + 8 * n], z8).astype(bf16)
-        far.append(send(qs.at[n], qr.at[n], at_tile(d)))
-
-    y = dot(triple("a0h"), part(0, "h", 0, 256))
-    x = dot(triple("a0l"), part(0, "l", 0, 256))
-    for n, v in enumerate((y[:64], y[64:128], x[:64])):
-        e0i[:, :, :, 1024 * n : 1024 * n + 1024] = (v * v).reshape(4, 2, 8, 1024)
-    pair0i = send(e0i.at[:, 1 - core], ce0i, partner)
-    y0e[:, 0:1024], y0e[:, 1024:2048], y0e[:, 2048:] = y[128:192], y[192:], x[64:]
-
+    for k in (1, 2):
+        down(k, 256, 288)
     gifts = [[], [], []]
 
     def give(k, n8, p8, gs, gr):
@@ -497,6 +501,14 @@
     give(2, y[8:16] + x[16:24], y[16:24] + x[24:32], gs2, gr2)
     ic[:, 0:256], ic[:, 256:384] = y[:8], x[:8, :128] + x[8:16, 128:]
 
+    wi = dot(const("wi"), stack34(256, 288))
+    ic[:, 384:] = wi[0:8]
+    z8 = jnp.zeros((8, 128), f32)
+    farther = []
+    for n, d in enumerate((1, -1, 2, -2, 3, -3, 4)):
+        gks[n] = wi[8 + 8 * n : 16 + 8 * n]
+        farther.append(send(gks.at[n], gkr.at[n], at_tile(d)))
+
     def fold(v):
         half = v.shape[1] // 2
         v = v * v
@@ -543,23 +555,25 @@
     for n, v in enumerate((q[:64], q[64:], x)):
         v = v + y1[:, 512 * n : 512 * n + 512]
         e1[:, :, :, 512 * n : 512 * n + 512] = (v * v).reshape(4, 2, 8, 512)
+    pair1 = send(e1.at[:, 1 - core], ce1, partner)
+
     g = got(2, hr2)
     v = yc[:, 0:256] + dot(const("u2h"), g)
-    e1[:, :, :, 1536:1792] = (v * v).reshape(4, 2, 8, 256)
+    ec[:, :, :, 0:256] = (v * v).reshape(4, 2, 8, 256)
     x = dot(const("u2l"), g)
     v = yc[:, 256:384] + x[:64, :128] + x[64:, 128:]
-    e1[:, :, :, 1792:1920] = (v * v).reshape(4, 2, 8, 128)
+    ec[:, :, :, 256:384] = (v * v).reshape(4, 2, 8, 128)
+    pair0e.wait_recv()
+    over0e = along_y(e0e, ce0e, es0e, er0e)
+    pair1.wait_recv()
+    over1 = along_y(e1, ce1, es1, er1)
     for copy in far:
         copy.wait_recv()
     q = qr[0].astype(f32) + qr[1].astype(f32) + qr[2].astype(f32)
-    v34 = kr[0] + kr[1] + (jr[0].astype(f32) + jr[1].astype(f32))[:72] + dot(const("x34"), rows(*split(q)))
-    v = yc[:, 384:] + v34[:64]
-    e1[:, :, :, 1920:] = (v * v).reshape(4, 2, 8, 128)
-    pair1 = send(e1.at[:, 1 - core], ce1, partner)
-
-    pair0e.wait_recv()
-    over0e = along_y(e0e, ce0e, es0e, er0e)
-
+    v34 = kr[0] + kr[1] + jr[0].astype(f32) + jr[1].astype(f32) + dot(const("x34"), rows(*split(q)))
+    v = yc[:, 384:] + v34
+    ec[:, :, :, 384:] = (v * v).reshape(4, 2, 8, 128)
+    pairc = send(ec.at[:, 1 - core], cec, partner)
     def taken(k, ref):
         for copy in gifts[k]:
             copy.wait_recv()
@@ -582,17 +596,17 @@
     ic[:, 0:256] += dot(const("u2hi"), g)
     x = dot(const("u2li"), g)
     ic[:, 256:384] += x[:8, :128] + x[8:, 128:]
-    ic[:, 384:] += v34[64:72]
-
-    pair1.wait_recv()
-    over1 = []
+    for copy in farther:
+        copy.wait_recv()
+    v = gkr[0] + gkr[1] + gkr[2] + gkr[3]
+    row = lax.broadcasted_iota(jnp.int32, (8, 128), 0)
+    ic[:, 384:] += v + jnp.where(row < 2, gkr[4] + gkr[5] + gkr[6], 0.0)
+    pairc.wait_recv()
+    overc = []
     for j in (2, 1, 3):
         q = lax.rem(ypos + j, 4)
-        both = e1[q, core] + ce1[q]
-        es2[j - 1] = both[:, 1536:]
-        over1.append(send(es2.at[j - 1], er2.at[j - 1], at_y(j)))
-        es1[j - 1] = fold(both[:, :1536])
-        over1.append(send(es1.at[j - 1], er1.at[j - 1], at_y(j)))
+        es2[j - 1] = ec[q, core] + cec[q]
+        overc.append(send(es2.at[j - 1], er2.at[j - 1], at_y(j)))
 
     need(COUNT + 2)
     w = [weights[i] * (1.0 / (MEM - 1)) for i in range(16)]
@@ -612,11 +626,11 @@
     ss0[1] = p0e[0:2]
     syn0 = [send(ss0.at[n], sr0.at[n], at_tile(d)) for n, d in enumerate((1, -1))]
 
-    v = e1[ypos, core] + ce1[ypos]
-    for copy in over1:
-        copy.wait_recv()
-    energy = v[:, 1536:] + er2[0] + er2[1] + er2[2]
-    row = lax.broadcasted_iota(jnp.int32, (8, 128), 0)
+    keep(p1, scaled(total(e1, ce1, er1, over1), i1, 1))
+    ss1[0] = p1[4:8]
+    ss1[1] = p1[0:4]
+    syn1 = [send(ss1.at[n], sr1.at[n], at_tile(d)) for n, d in enumerate(NEXT)]
+
     lane = lax.broadcasted_iota(jnp.int32, (8, 128), 1)
     w34 = jnp.where(
         row < 2,
@@ -624,16 +638,12 @@
         jnp.where(row < 4, w[9], jnp.where(row < 6, w[11], w[10])),
     )
     w2 = jnp.where(lax.broadcasted_iota(jnp.int32, (8, 256), 0) < 4, w[6], w[8])
-    pc[:, 0:256] = w2 * energy[:, 0:256] * ic[:, 0:256]
-    pc[:, 256:384] = w[7] * energy[:, 256:384] * ic[:, 256:384]
-    pc[:, 384:] = w34 * energy[:, 384:] * ic[:, 384:]
-    synt = [send(pc.at[:, 384:], srt.at[n], at_tile(d)) for n, d in enumerate((2, -2, 3, -3, -4))]
-    sync = [send(pc, syc.at[n], at_tile(d)) for n, d in enumerate((1, -1))]
-    energy = v[:, :1536] + unfold(er1[0]) + unfold(er1[1]) + unfold(er1[2])
-    keep(p1, scaled(energy, i1, 1))
-    ss1[0] = p1[4:8]
-    ss1[1] = p1[0:4]
-    syn1 = [send(ss1.at[n], sr1.at[n], at_tile(d)) for n, d in enumerate((1, -1))]
+    v = ec[ypos, core] + cec[ypos]
+    for copy in overc:
+        copy.wait_recv()
+    pc[...] = lanes(w2, jnp.full((8, 128), w[7]), w34) * (v + er2[0] + er2[1] + er2[2]) * ic[...]
+    sync = [send(pc.at[:, 384:], srt.at[n], at_tile(d)) for n, d in enumerate(FAR)]
+    sync += [send(pc, syc.at[n], at_tile(d)) for n, d in enumerate(NEXT)]
 
     bi = const("bi")
     bi_hi, bi_lo = bi[:768], bi[768:]
@@ -642,46 +652,44 @@
         hi, lo = split(x)
         return dot(const(name), rows(hi, lo, hi))
 
-    def columns(x):
-        tall, half = x.shape[0], x.shape[1] // 2
+    def columns(x, sides=2):
+        tall, half = x.shape[0], x.shape[1] // sides
         count = half // 128
+        starts = (0, half)[:sides]
 
         def win(j):
-            return lanes(*[x[:, s + 128 * ((j + i) % count) : s + 128 * ((j + i) % count) + 128] for s in (0, half) for i in (-1, 0, 1)])
+            return lanes(*[x[:, s + 128 * ((j + i) % count) : s + 128 * ((j + i) % count) + 128] for s in starts for i in (-1, 0, 1)])
 
         a, b = split(rows(*[win(j) for j in range(count)]))
-        r = dot(rows(a, b), bi_hi)
-        r = r[: tall * count] + r[tall * count :] + dot(a, bi_lo)
+        r = dot(rows(a, b), bi_hi[: 384 * sides])
+        r = r[: tall * count] + r[tall * count :] + dot(a, bi_lo[: 384 * sides])
         return lanes(*[r[tall * j : tall * j + tall] for j in range(count)])
 
-    for copy in synt + sync:
+    for copy in syn0:
         copy.wait_recv()
-    t = {-2: srt[0], 2: srt[1], -3: srt[2], 3: srt[3], 4: srt[4], 0: pc[:, 384:], -1: syc[0, :, 384:], 1: syc[1, :, 384:]}
-    stack = rows(*[t[b] for b in range(-3, 5)])
-    hi, lo = split(left("s4", stack))
-    m = const("i4")
-    ll3 = dot(hi, m[:128]) + dot(lo, m[:128]) + dot(hi, m[128:])
-    ll2 = columns(lanes(left("s3l", rows(stack, ll3, z8)), left("s3h", stack)))
-    stack = rows(syc[0, :, 0:384], pc[:, 0:384], syc[1, :, 0:384], jnp.zeros((8, 384), f32))
-    ll1 = columns(lanes(
-        left("s2l0", rows(stack[:, 256:384], ll2[:, :128])),
-        left("s2l1", rows(stack[:, 256:384], ll2[:, 128:])),
-        left("s2h", stack[:, :256]),
-    ))
+    stack = rows(p0i[...], p0e[...], sr0[0], sr0[1], jnp.zeros((12, 3072), f32))
+    out[...] = columns(lanes(left("s0p", stack[:, 2048:]), left("s0h", rows(stack[:, 0:1024], stack[:, 1024:2048]))))
     for copy in syn1:
         copy.wait_recv()
     stack = rows(p1[...], sr1[0], sr1[1])
-    ll0 = columns(lanes(
-        left("s1l", rows(ll1, stack[:, 1024:])),
-        left("s1h", rows(stack[:, 0:512], stack[:, 512:1024])),
-    ))
-    for copy in syn0:
+    base0 = columns(lanes(left("s1p", stack[:, 1024:]), left("s1h", rows(stack[:, 0:512], stack[:, 512:1024]))))
+
+    for copy in sync:
         copy.wait_recv()
-    stack = rows(p0i[...], p0e[...], sr0[0], sr0[1], jnp.zeros((4, 3072), f32))
-    out[...] = columns(lanes(
-        left("s0l", rows(ll0, stack[:, 2048:])),
-        left("s0h", rows(stack[:, 0:1024], stack[:, 1024:2048])),
-    ))
+    own, beside = pc[...], [syc[0], syc[1]]
+    t = {0: own[:, 384:], -1: beside[0][:, 384:], 1: beside[1][:, 384:]}
+    for n, d in enumerate(FAR):
+        t[-d] = srt[n]
+    x = left("s34", rows(*[t[b] for b in range(-3, 5)]))
+    hi, lo = split(lanes(x[:16], x[16:32], x[32:]))
+    m = const("i34")
+    ll2 = dot(hi, m[:384]) + dot(lo, m[:384]) + dot(hi, m[384:])
+    stack = rows(beside[0][:, 0:384], own[:, 0:384], beside[1][:, 0:384], jnp.zeros((8, 384), f32))
+    x = left("s2p", stack[:, 256:])
+    base1 = columns(lanes(x[:16], x[16:], left("s2h", stack[:, :256])))
+    ll1 = base1 + columns(left("s2x", ll2), 1)
+    ll0 = base0 + columns(left("s1x", ll1), 1)
+    out[...] += columns(left("s0x", rows(ll0, jnp.zeros((8, 1024), f32))), 1)
     for copy in sent:
         copy.wait_send()
 
@@ -692,26 +700,27 @@
     v = pltpu.VMEM
     scratch = [v(a.shape, bf16) for a in arrays] + [
         v((256, 2048), bf16), v((BAND, 2048), f32), pltpu.SMEM((16,), f32),
-        v((288, 3968), bf16), v((288, 3968), bf16), v((128, 2048), bf16), v((128, 2048), bf16), v((32, 2048), bf16), v((32, 2048), bf16),
-        v((8, 128), f32), v((64, 3072), f32), v((64, 1536), f32), v((64, 512), f32),
+        v((288, 3584), bf16), v((288, 3584), bf16), v((128, 2048), bf16), v((128, 2048), bf16), v((32, 2048), bf16), v((32, 2048), bf16),
+        v((64, 3072), f32), v((64, 1536), f32), v((64, 512), f32),
         v((8, 3072), f32), v((8, 3072), f32), v((8, 1536), f32), v((8, 512), f32),
         v((2, 32, 1024), bf16), v((2, 48, 512), bf16), v((2, 64, 256), bf16),
         v((2, 32, 1024), bf16), v((2, 48, 512), bf16), v((2, 64, 256), bf16),
         v((2, 4, 1024), f32), v((2, 8, 512), f32), v((2, 8, 256), f32),
         v((2, 4, 1024), f32), v((2, 8, 512), f32), v((2, 8, 256), f32),
-        v((2, 72, 128), f32), v((2, 72, 128), f32), v((2, 80, 128), bf16), v((2, 80, 128), bf16), v((3, 32, 128), bf16), v((3, 32, 128), bf16),
-        v((4, 2, 8, 3072), f32), v((4, 2, 8, 3072), f32), v((4, 2, 8, 2048), f32),
-        v((4, 8, 3072), f32), v((4, 8, 3072), f32), v((4, 8, 2048), f32),
+        v((2, 64, 128), f32), v((2, 64, 128), f32), v((2, 64, 128), bf16), v((2, 64, 128), bf16), v((3, 16, 128), bf16), v((3, 16, 128), bf16),
+        v((7, 8, 128), f32), v((7, 8, 128), f32),
+        v((4, 2, 8, 3072), f32), v((4, 2, 8, 3072), f32), v((4, 2, 8, 1536), f32), v((4, 2, 8, 512), f32),
+        v((4, 8, 3072), f32), v((4, 8, 3072), f32), v((4, 8, 1536), f32), v((4, 8, 512), f32),
         v((3, 16, 1536), bf16), v((3, 16, 1536), bf16), v((3, 16, 768), bf16), v((3, 8, 512), f32),
         v((3, 16, 1536), bf16), v((3, 16, 1536), bf16), v((3, 16, 768), bf16), v((3, 8, 512), f32),
+        v((2, 8, 512), f32), v((5, 8, 128), f32),
         v((8, 3072), f32), v((8, 3072), f32), v((8, 1536), f32), v((8, 512), f32),
         v((2, 2, 3072), f32), v((2, 4, 1536), f32), v((2, 2, 3072), f32), v((2, 4, 1536), f32),
-        v((2, 8, 512), f32), v((5, 8, 128), f32),
-        pltpu.SemaphoreType.DMA((48,)), pltpu.SemaphoreType.DMA((48,)), pltpu.SemaphoreType.DMA((COUNT + 3,)),
+        pltpu.SemaphoreType.DMA((96,)), pltpu.SemaphoreType.DMA((96,)), pltpu.SemaphoreType.DMA((COUNT + 3,)),
     ]
     result = pl.pallas_call(
         kernel,
-        out_shape=jax.ShapeDtypeStruct((BAND, 2048), f32),
+        out_shape=pltpu.VMEM((BAND, 2048), f32),
         in_specs=[anywhere] * (3 + COUNT),
         out_specs=pl.BlockSpec(memory_space=pltpu.VMEM),
         scratch_shapes=scratch,

time: 36.6 us -> 35.7 us (0.975)
  local copies, waits for them, and re-layouts: 1.67 us -> 0.71 us
    unnamed x1, local copies, waits for them, and re-layouts: 1.67 us -> 0.71 us
where the time goes in v3:
time: 35.7 us; the launch traced here: 35.6 us
  Pallas kernels  34.9 us (98%)
  local copies, waits for them, and re-layouts  0.71 us (2%)
    pallas_call x1, Pallas kernels, local(): pl.pallas_call(kernel, out_shape=pltpu.VMEM((BAND, 2048), f32), in_specs=...  34.9 us

profile of v3, /device:TPU:1, one launch (start us, length us, event | category | flops | bytes accessed | tf_op | source)
XLA Modules:
  0.0 35.6 jit_solution(13875827245859489582)
XLA Ops:
  0.0 34.9 %shard_map.109 = f32[32,2048]{1,0:T(8,128)S(1)} custom-call(bf16[256,2048]{1,0:T(8,128)(2,1)} %bitcast.4, f32[32,2048]{1,0:T(8,128)} %bitcast.5, f32[16]{0:T(128)} %weights_hbm.1, bf16[1024,256]{1,0:T(8,128)(2,1)} %constant.16.clone.refs_0_, bf16[1184,512]{1,0:T(8,128)(2,1)} %constant.17.clone.refs_1_, bf16[368,1536]{1,0:T(8,128)(2,1)} %constant.18.clone.refs_2_, ...), custom_call_target="tpu_custom_call" | custom-call | tf_op jit(solution)/shard_map/pallas_call | solution.py:721
  34.9 0.7 %copy.13 = f32[1,32,2048]{2,1,0:T(8,128)} copy(f32[1,32,2048]{2,1,0:T(8,128)S(1)} %bitcast.3) | data formatting | bytes 524288

commit v4 on v3

--- a/solution.py
+++ b/solution.py
@@ -326,8 +326,6 @@
     partner = (ypos * 2 + 1 - core, tile)
     near = [at_tile(d) for d in (1, -1, 2, -2, 3, -3, 4, -4)] + [partner] + [at_y(j) for j in (1, 2, 3)]
     barrier = pltpu.get_barrier_semaphore()
-    for device in near:
-        pl.semaphore_signal(barrier, inc=1, device_id=device, device_id_type=MESH)
 
     sources = [(groups_hbm[0], groups[0]), (members_hbm, members), (increment_hbm, increment)]
     sources += [(groups_hbm[g], groups[g]) for g in range(1, COUNT)] + [(weights_hbm, weights)]
@@ -386,6 +384,8 @@
 
     base = [0, 2048, 3072]
     begin(0, 1)
+    for device in near:
+        pl.semaphore_signal(barrier, inc=1, device_id=device, device_id_type=MESH)
     bf = const("bf")
     bf_hi, bf_lo = bf[:512], bf[512:]
     need(1)
@@ -432,7 +432,6 @@
     down(1, 0, 256)
     share(1, dot(triple("a1h")[128:], part(1, "h", 0, 256)), dot(triple("a1l")[64:], part(1, "l", 0, 256)), hs1, hr1)
     down(2, 0, 256)
-    share(2, dot(triple("a2h")[64:], part(2, "h", 0, 256)), dot(triple("a2l")[128:], part(2, "l", 0, 256)), hs2, hr2)
 
     def stack34(first, last):
         m, s = const("b34"), base[2]
@@ -453,6 +452,8 @@
     for n, d in enumerate((3, -3, 4)):
         qs[n] = wm[320 + 16 * n : 336 + 16 * n].astype(bf16)
         far.append(send(qs.at[n], qr.at[n], at_tile(d)))
+
+    share(2, dot(triple("a2h")[64:], part(2, "h", 0, 256)), dot(triple("a2l")[128:], part(2, "l", 0, 256)), hs2, hr2)
 
     y = dot(triple("a0h"), part(0, "h", 0, 256))
     x = dot(triple("a0l"), part(0, "l", 0, 256))
@@ -674,6 +675,8 @@
     stack = rows(p1[...], sr1[0], sr1[1])
     base0 = columns(lanes(left("s1p", stack[:, 1024:]), left("s1h", rows(stack[:, 0:512], stack[:, 512:1024]))))
 
+    for copy in sent:
+        copy.wait_send()
     for copy in sync:
         copy.wait_recv()
     own, beside = pc[...], [syc[0], syc[1]]
@@ -690,8 +693,6 @@
     ll1 = base1 + columns(left("s2x", ll2), 1)
     ll0 = base0 + columns(left("s1x", ll1), 1)
     out[...] += columns(left("s0x", rows(ll0, jnp.zeros((8, 1024), f32))), 1)
-    for copy in sent:
-        copy.wait_send()
 
 
 def local(members, increment, weights):

time: 35.7 us -> 35.6 us (level)
  no operation moved by 1% of the time
where the time goes in v4:
time: 35.6 us; the launch traced here: 35.5 us
  Pallas kernels  34.8 us (98%)
  local copies, waits for them, and re-layouts  0.71 us (2%)
    pallas_call x1, Pallas kernels, local(): pl.pallas_call(kernel, out_shape=pltpu.VMEM((BAND, 2048), f32), in_specs=...  34.8 us

profile of v4, /device:TPU:1, one launch (start us, length us, event | category | flops | bytes accessed | tf_op | source)
XLA Modules:
  0.0 35.5 jit_solution(7495263904965467408)
XLA Ops:
  0.0 34.8 %shard_map.109 = f32[32,2048]{1,0:T(8,128)S(1)} custom-call(bf16[256,2048]{1,0:T(8,128)(2,1)} %bitcast.4, f32[32,2048]{1,0:T(8,128)} %bitcast.5, f32[16]{0:T(128)} %weights_hbm.1, bf16[1024,256]{1,0:T(8,128)(2,1)} %constant.16.clone.refs_0_, bf16[1184,512]{1,0:T(8,128)(2,1)} %constant.17.clone.refs_1_, bf16[368,1536]{1,0:T(8,128)(2,1)} %constant.18.clone.refs_2_, ...), custom_call_target="tpu_custom_call" | custom-call | tf_op jit(solution)/shard_map/pallas_call | solution.py:722
  34.8 0.7 %copy.13 = f32[1,32,2048]{2,1,0:T(8,128)} copy(f32[1,32,2048]{2,1,0:T(8,128)S(1)} %bitcast.3) | data formatting | bytes 524288

commit v5 on v4

--- a/solution.py
+++ b/solution.py
@@ -96,7 +96,8 @@
     bi = np.concatenate([s2048[1024:1280, 384:768], s2048[1024:1280, 1024 + 384 : 1024 + 768]], axis=1).T
     c["bi"] = np.concatenate(pieces(bi), axis=0)
     s256 = inverse_matrix(256).T
-    c["i34"] = np.concatenate(pieces(np.concatenate([inverse_matrix(128).T @ s256[:128], s256], axis=0)), axis=0)
+    s512 = inverse_matrix(512).T[:256]
+    c["i34"] = np.concatenate(pieces(np.concatenate([inverse_matrix(128).T @ s256[:128], s256], axis=0) @ s512), axis=0)
 
     inner, edge = list(range(4, 12)), [0, 1, 2, 3, 12, 13, 14, 15]
     for k in range(3):
@@ -193,9 +194,6 @@
         assert np.abs(tile34(-4)).max() == 0 and np.abs(tile34(5)).max() == 0 and np.abs(tile34(-5)).max() == 0
         m = np.concatenate(out, axis=0)
         c[f"w{tag}"] = halves(m) if f == 8 else three(m)
-    spread = np.kron(np.eye(8), np.eye(8)[:, :2])
-    c["x34"] = np.concatenate([spread, spread], axis=1).astype(bf16)
-
     def pick(k, start, stop, rows_out, low_slots, high_slots):
         n = NROW >> k
         m = inverse_matrix(n)
@@ -228,15 +226,15 @@
     h3 = flat([none * 4 + [2 * b, 2 * b + 1] + none * 2 for b in bands])
     h3l = flat([none * 6 + [2 * b, 2 * b + 1] for b in bands])
     low3 = pick(3, -2, 8, 16, list(range(-2, 6)), none * 8)
-    c["s34"] = three(np.concatenate([low3 @ m4, pick(3, -2, 8, 16, none * 64, h3l), pick(3, -2, 8, 16, l3, h3)], axis=0))
+    low_ext = [-2 + i if i < 10 else None for i in range(16)]
+    low2 = pick(2, -2, 12, 16, low_ext, none * 16)
+    c["s34"] = three(np.concatenate([low2 @ low3 @ m4, low2 @ pick(3, -2, 8, 16, none * 64, h3l), low2 @ pick(3, -2, 8, 16, l3, h3)], axis=0))
     near = (-1, 0, 1)
     l2 = flat([[4 * b + i for i in range(4)] + none * 4 for b in near]) + none * 8
     h2 = flat([none * 4 + [4 * b + i for i in range(4)] for b in near]) + none * 8
     c["s2h"] = three(pick(2, -2, 12, 16, l2, h2))
-    low_ext = [-2 + i if i < 10 else None for i in range(16)]
     ha = flat([[4 * b + i for i in range(4)] + none * 4 for b in near]) + none * 8
     hb = flat([none * 4 + [4 * b + i for i in range(4)] for b in near]) + none * 8
-    c["s2x"] = three(pick(2, -2, 12, 16, low_ext, none * 16))
     c["s2p"] = three(np.concatenate([pick(2, -2, 12, 16, none * 32, ha), pick(2, -2, 12, 16, none * 32, hb)], axis=0))
     s1 = list(range(8)) + list(range(-4, 0)) + list(range(8, 12))
     c["s1h"] = three(pick(1, -2, 18, 24, s1 + none * 16, none * 16 + s1))
@@ -257,9 +255,10 @@
     ("wm",),
     ("a0h", "a0l"),
     ("a0hi", "a0li", "a1hi", "a1li", "a2hi", "a2li", "wi"),
-    ("u0h", "u0l", "u1h", "u1l", "u2h", "u2l", "x34", "u0hi", "u0li", "u1hi", "u1li", "u2hi", "u2li"),
-    ("i34", "s34", "s2h", "s2x", "s2p", "s1h", "s1x", "s1p", "s0h", "s0x", "s0p"),
+    ("u0h", "u0l", "u1h", "u1l", "u2h", "u2l", "u0hi", "u0li", "u1hi", "u1li", "u2hi", "u2li"),
+    ("s34", "s2h", "s2p", "s1h", "s1x", "s1p", "s0h", "s0x", "s0p"),
     ("bi",),
+    ("i34",),
 )
 
 
@@ -310,7 +309,7 @@
      y0e, y1, yc, i0i, i0e, i1, ic,
      hs0, hs1, hs2, hr0, hr1, hr2, gs0, gs1, gs2, gr0, gr1, gr2,
      ks, kr, js, jr, qs, qr, gks, gkr,
-     e0i, e0e, e1, ec, ce0i, ce0e, ce1, cec, es0i, es0e, es1, es2, er0i, er0e, er1, er2,
+     e0i, e0e, e1, ec, ce0i, ce0e, ce1, es0i, es0e, es1, er0i, er0e, er1, er2,
      syc, srt, p0i, p0e, p1, pc, ss0, ss1, sr0, sr1,
      sem_s, sem_r, sem_l) = refs[2 * COUNT + 1 :]
     where = packed()[1]
@@ -323,8 +322,11 @@
     def at_y(j):
         return (lax.rem(ypos + j, 4) * 2 + core, tile)
 
+    def at_mem(j):
+        return (lax.rem(mem + j, MEM), tile)
+
     partner = (ypos * 2 + 1 - core, tile)
-    near = [at_tile(d) for d in (1, -1, 2, -2, 3, -3, 4, -4)] + [partner] + [at_y(j) for j in (1, 2, 3)]
+    near = [at_tile(d) for d in (1, -1, 2, -2, 3, -3, 4, -4)] + [at_mem(j) for j in range(1, MEM)]
     barrier = pltpu.get_barrier_semaphore()
 
     sources = [(groups_hbm[0], groups[0]), (members_hbm, members), (increment_hbm, increment)]
@@ -571,10 +573,16 @@
     for copy in far:
         copy.wait_recv()
     q = qr[0].astype(f32) + qr[1].astype(f32) + qr[2].astype(f32)
-    v34 = kr[0] + kr[1] + jr[0].astype(f32) + jr[1].astype(f32) + dot(const("x34"), rows(*split(q)))
-    v = yc[:, 384:] + v34
+    v34 = kr[0] + kr[1] + jr[0].astype(f32) + jr[1].astype(f32)
+    yc[:, 384:] += v34
+    for n in range(8):
+        yc[8 * n : 8 * n + 2, 384:] += q[2 * n : 2 * n + 2]
+    v = yc[:, 384:]
     ec[:, :, :, 384:] = (v * v).reshape(4, 2, 8, 128)
-    pairc = send(ec.at[:, 1 - core], cec, partner)
+    overc = []
+    for j in (4, 3, 5, 2, 6, 1, 7):
+        owner = lax.rem(mem + j, MEM)
+        overc.append(send(ec.at[lax.div(owner, 2), lax.rem(owner, 2)], er2.at[j - 1], at_mem(j)))
     def taken(k, ref):
         for copy in gifts[k]:
             copy.wait_recv()
@@ -602,13 +610,6 @@
     v = gkr[0] + gkr[1] + gkr[2] + gkr[3]
     row = lax.broadcasted_iota(jnp.int32, (8, 128), 0)
     ic[:, 384:] += v + jnp.where(row < 2, gkr[4] + gkr[5] + gkr[6], 0.0)
-    pairc.wait_recv()
-    overc = []
-    for j in (2, 1, 3):
-        q = lax.rem(ypos + j, 4)
-        es2[j - 1] = ec[q, core] + cec[q]
-        overc.append(send(es2.at[j - 1], er2.at[j - 1], at_y(j)))
-
     need(COUNT + 2)
     w = [weights[i] * (1.0 / (MEM - 1)) for i in range(16)]
 
@@ -639,10 +640,12 @@
         jnp.where(row < 4, w[9], jnp.where(row < 6, w[11], w[10])),
     )
     w2 = jnp.where(lax.broadcasted_iota(jnp.int32, (8, 256), 0) < 4, w[6], w[8])
-    v = ec[ypos, core] + cec[ypos]
+    v = ec[ypos, core]
     for copy in overc:
         copy.wait_recv()
-    pc[...] = lanes(w2, jnp.full((8, 128), w[7]), w34) * (v + er2[0] + er2[1] + er2[2]) * ic[...]
+    for n in range(MEM - 1):
+        v = v + er2[n]
+    pc[...] = lanes(w2, jnp.full((8, 128), w[7]), w34) * v * ic[...]
     sync = [send(pc.at[:, 384:], srt.at[n], at_tile(d)) for n, d in enumerate(FAR)]
     sync += [send(pc, syc.at[n], at_tile(d)) for n, d in enumerate(NEXT)]
 
@@ -686,11 +689,11 @@
     x = left("s34", rows(*[t[b] for b in range(-3, 5)]))
     hi, lo = split(lanes(x[:16], x[16:32], x[32:]))
     m = const("i34")
-    ll2 = dot(hi, m[:384]) + dot(lo, m[:384]) + dot(hi, m[384:])
+    ll1 = dot(hi, m[:384]) + dot(lo, m[:384]) + dot(hi, m[384:])
     stack = rows(beside[0][:, 0:384], own[:, 0:384], beside[1][:, 0:384], jnp.zeros((8, 384), f32))
     x = left("s2p", stack[:, 256:])
     base1 = columns(lanes(x[:16], x[16:], left("s2h", stack[:, :256])))
-    ll1 = base1 + columns(left("s2x", ll2), 1)
+    ll1 = ll1 + base1
     ll0 = base0 + columns(left("s1x", ll1), 1)
     out[...] += columns(left("s0x", rows(ll0, jnp.zeros((8, 1024), f32))), 1)
 
@@ -711,9 +714,9 @@
         v((2, 64, 128), f32), v((2, 64, 128), f32), v((2, 64, 128), bf16), v((2, 64, 128), bf16), v((3, 16, 128), bf16), v((3, 16, 128), bf16),
         v((7, 8, 128), f32), v((7, 8, 128), f32),
         v((4, 2, 8, 3072), f32), v((4, 2, 8, 3072), f32), v((4, 2, 8, 1536), f32), v((4, 2, 8, 512), f32),
-        v((4, 8, 3072), f32), v((4, 8, 3072), f32), v((4, 8, 1536), f32), v((4, 8, 512), f32),
-        v((3, 16, 1536), bf16), v((3, 16, 1536), bf16), v((3, 16, 768), bf16), v((3, 8, 512), f32),
-        v((3, 16, 1536), bf16), v((3, 16, 1536), bf16), v((3, 16, 768), bf16), v((3, 8, 512), f32),
+        v((4, 8, 3072), f32), v((4, 8, 3072), f32), v((4, 8, 1536), f32),
+        v((3, 16, 1536), bf16), v((3, 16, 1536), bf16), v((3, 16, 768), bf16),
+        v((3, 16, 1536), bf16), v((3, 16, 1536), bf16), v((3, 16, 768), bf16), v((MEM - 1, 8, 512), f32),
         v((2, 8, 512), f32), v((5, 8, 128), f32),
         v((8, 3072), f32), v((8, 3072), f32), v((8, 1536), f32), v((8, 512), f32),
         v((2, 2, 3072), f32), v((2, 4, 1536), f32), v((2, 2, 3072), f32), v((2, 4, 1536), f32),

time: 35.6 us -> 35.5 us (level)
  no operation moved by 1% of the time
where the time goes in v5:
time: 35.5 us; the launch traced here: 35.4 us
  Pallas kernels  34.7 us (98%)
  local copies, waits for them, and re-layouts  0.71 us (2%)
    pallas_call x1, Pallas kernels, local(): pl.pallas_call(kernel, out_shape=pltpu.VMEM((BAND, 2048), f32), in_specs=...  34.7 us

profile of v5, /device:TPU:1, one launch (start us, length us, event | category | flops | bytes accessed | tf_op | source)
XLA Modules:
  0.0 35.4 jit_solution(1656672102920808746)
XLA Ops:
  0.0 34.7 %shard_map.118 = f32[32,2048]{1,0:T(8,128)S(1)} custom-call(bf16[256,2048]{1,0:T(8,128)(2,1)} %bitcast.4, f32[32,2048]{1,0:T(8,128)} %bitcast.5, f32[16]{0:T(128)} %weights_hbm.1, bf16[1024,256]{1,0:T(8,128)(2,1)} %constant.18.clone.refs_0_, bf16[1184,512]{1,0:T(8,128)(2,1)} %constant.19.clone.refs_1_, bf16[368,1536]{1,0:T(8,128)(2,1)} %constant.20.clone.refs_2_, ...), custom_call_target="tpu_custom_call" | custom-call | tf_op jit(solution)/shard_map/pallas_call | solution.py:725
  34.7 0.7 %copy.14 = f32[1,32,2048]{2,1,0:T(8,128)} copy(f32[1,32,2048]{2,1,0:T(8,128)S(1)} %bitcast.3) | data formatting | bytes 524288
